TPU v7x, 256 devices: a whole 4x4x8 slice. The times are simulated.
256 devices in a mesh: wave: 128 (over z, y, x), lev: 2 (over core).
Axes of the slice: x: 4, y: 4, z: 8, core: 2. Of those that a mesh axis runs over, the one named last changes fastest.
Arguments:
- fourier: bfloat16 [2, 2, 4, 2560, 1280], P(None, None, 'lev', 'wave'), may hold values from -6 to 6
- lat_rows: int32 [2560], replicated, may hold values from 0 to 2559, each once
- wave_slots: int32 [1280], replicated, may hold values from 0 to 1279, as said below
- pressure_balance_operator: float32 [4, 4], replicated, may hold values from -3 to 3
- depths: float32 [4], replicated, may hold values from 0.05 to 5
- vertical_modes: float32 [4, 4], replicated, may hold values from -3 to 3
- mode_projection: float32 [4, 4], replicated, may hold values from -3 to 3
- heat_link_operator: float32 [4, 4], replicated, may hold values from -3 to 3
Outputs:
- spectral_state: bfloat16 [1280, 2, 2, 4, 1280], P('wave', None, None, 'lev')
- grid_field: bfloat16 [2, 2, 4, 2560, 1280], P(None, None, 'lev', 'wave')
Inputs may be any that keep to these rules, and one draw needn't show every extreme that they name: `lat_rows`: each latitude appears once. `wave_slots`: each wavenumber appears once; entry 2 i is below 640 and entry 2 i + 1 equals 1279 minus entry 2 i.
All inputs are finite; a program needn't handle non-finite values.
Results may differ from a plain program's by a relative error of at most 0.011.
Values may be sent and summed in bfloat16 or wider, within the bound.
A program may use at most 192 MiB of HBM per device.

v0:
```python
import math

import jax
import jax.numpy as jnp
from jax import lax
from jax.sharding import PartitionSpec as P


def geometry(lat_count):
    hemisphere = lat_count // 2
    colatitude = jnp.pi * (jnp.arange(hemisphere, dtype=jnp.float32) + 0.5) / lat_count
    sine_row = jnp.sin(colatitude)
    return (jnp.cos(colatitude), sine_row, math.sqrt(math.pi / lat_count) * sine_row)


def legendre_tables(orders, cosine_row, sine_row, table_length, wave_count):
    degree_base = orders.astype(jnp.float32)[:, None]
    constant = 0.5 * math.log(math.pi)
    log_scale = (
        0.5 * (lax.lgamma(degree_base + 1.5) - lax.lgamma(degree_base + 1.0) - constant)
        + degree_base * jnp.log(sine_row)[None, :]
    )
    former = jnp.zeros_like(log_scale)
    current = jnp.ones_like(log_scale)
    cosine_grid = cosine_row[None, :]

    def block_step(state_carry, block_start):
        former, current, log_scale = state_carry
        even_rows = []
        odd_rows = []
        for offset in range(64):
            degree = degree_base + (block_start + offset).astype(jnp.float32)
            entry_value = jnp.where(degree < wave_count, current * jnp.exp(log_scale), 0.0)
            if offset % 2 == 0:
                even_rows.append(entry_value.astype(jnp.bfloat16))
            else:
                odd_rows.append(entry_value.astype(jnp.bfloat16))
            next_degree = degree + 1.0
            grow_factor = jnp.sqrt(
                (4.0 * next_degree * next_degree - 1.0)
                / (next_degree * next_degree - degree_base * degree_base)
            )
            damp_factor = jnp.sqrt(
                (degree * degree - degree_base * degree_base) / (4.0 * degree * degree - 1.0)
            )
            following = grow_factor * (cosine_grid * current - damp_factor * former)
            former, current = (current, following)
            if offset % 8 == 7:
                magnitude = jnp.sqrt(former * former + current * current)
                former = former / magnitude
                current = current / magnitude
                log_scale = log_scale + jnp.log(magnitude)
        return ((former, current, log_scale), (jnp.stack(even_rows), jnp.stack(odd_rows)))

    block_starts = jnp.arange(table_length // 64, dtype=jnp.int32) * 64
    _, (even_table, odd_table) = lax.scan(block_step, (former, current, log_scale), block_starts)
    part_shape = (table_length // 2,) + log_scale.shape
    return (even_table.reshape(part_shape), odd_table.reshape(part_shape))


def coupling_table(orders, table_length, wave_count):
    degree = (orders[:, None] + jnp.arange(table_length, dtype=jnp.int32)[None, :]).astype(
        jnp.float32
    )
    return degree * (degree + 1.0) / float(wave_count * wave_count)


def vertical(harmonic_amplitudes, orders, matrices, wave_count):
    pressure_balance_operator, depths, vertical_modes, mode_projection, heat_link_operator = (
        matrices
    )
    maximal_legendre_order = lax.Precision.HIGHEST
    column_link_operator = coupling_table(orders, harmonic_amplitudes.shape[4], wave_count)[
        :, None, None, :
    ]
    flow_spreading_grid = harmonic_amplitudes[:, :, 0]
    heat_grid_values = harmonic_amplitudes[:, :, 1]
    forcing_vector = flow_spreading_grid + column_link_operator * jnp.einsum(
        "re,cney->cnry",
        pressure_balance_operator,
        heat_grid_values,
        precision=maximal_legendre_order,
    )
    projected = jnp.einsum(
        "re,cney->cnry", mode_projection, forcing_vector, precision=maximal_legendre_order
    )
    scaled = projected / (1.0 + column_link_operator * depths[None, None, :, None])
    flow_spreading_next = jnp.einsum(
        "va,mrak->mrvk", vertical_modes, scaled, precision=maximal_legendre_order
    )
    heat_values_next = heat_grid_values - jnp.einsum(
        "re,cney->cnry", heat_link_operator, flow_spreading_next, precision=maximal_legendre_order
    )
    return jnp.stack([flow_spreading_next, heat_values_next], axis=2)


def fold_rows(received, north_rows, south_rows, weight_row):
    upper_half = jnp.take(received, north_rows, axis=4).astype(jnp.float32)
    lower_half = jnp.take(received, south_rows, axis=4).astype(jnp.float32)
    return (
        ((upper_half + lower_half) * weight_row).astype(jnp.bfloat16),
        ((upper_half - lower_half) * weight_row).astype(jnp.bfloat16),
    )


def analyze(symmetric, antisymmetric, tables):
    even_table, odd_table = tables
    even_part = jnp.einsum(
        "mrfvh,kmh->mrfvk", symmetric, even_table, preferred_element_type=jnp.float32
    )
    odd_part = jnp.einsum(
        "mrfvh,kmh->mrfvk", antisymmetric, odd_table, preferred_element_type=jnp.float32
    )
    return jnp.stack([even_part, odd_part], axis=-1).reshape(
        even_part.shape[:4] + (2 * even_part.shape[4],)
    )


def unfold_rows(updated, tables, mirror_index, mirror_sign, inverse_scale):
    even_table, odd_table = tables
    folded_sym = jnp.einsum(
        "mrfvk,kmh->mrfvh", updated[..., 0::2], even_table, preferred_element_type=jnp.float32
    )
    folded_anti = jnp.einsum(
        "mrfvk,kmh->mrfvh", updated[..., 1::2], odd_table, preferred_element_type=jnp.float32
    )
    row_values = jnp.take(folded_sym, mirror_index, axis=4) + mirror_sign * jnp.take(
        folded_anti, mirror_index, axis=4
    )
    return (row_values * inverse_scale).astype(jnp.bfloat16)


def body(
    fourier,
    lat_rows,
    wave_slots,
    pressure_balance_operator,
    depths,
    vertical_modes,
    mode_projection,
    heat_link_operator,
):
    wave_count = fourier.shape[4]
    lat_count = lat_rows.shape[0]
    hemisphere = lat_count // 2
    wave_devices = lax.axis_size("wave")
    level_devices = lax.axis_size("lev")
    per_device = wave_count // wave_devices
    cosine_row, sine_row, weight_row = geometry(lat_count)
    position = (
        jnp.zeros((lat_count,), jnp.int32).at[lat_rows].set(jnp.arange(lat_count, dtype=jnp.int32))
    )
    north_rows = position[:hemisphere]
    south_rows = position[::-1][:hemisphere]
    mirror_index = jnp.minimum(lat_rows, lat_count - 1 - lat_rows)
    mirror_sign = jnp.where(lat_rows < hemisphere, 1.0, -1.0).astype(jnp.float32)
    inverse_scale = 1.0 / math.sqrt(wave_count)
    wave_index = lax.axis_index("wave")
    level_index = lax.axis_index("lev")
    slot_numbers = (
        jnp.zeros((wave_count,), jnp.int32)
        .at[wave_slots]
        .set(jnp.arange(wave_count, dtype=jnp.int32))
    )
    arranged = jnp.transpose(jnp.take(fourier, wave_slots, axis=4), (4, 0, 1, 2, 3))
    matrices = (
        pressure_balance_operator,
        depths,
        vertical_modes,
        mode_projection,
        heat_link_operator,
    )
    slot_count = per_device // level_devices
    orders = lax.dynamic_slice_in_dim(
        wave_slots, wave_index * per_device + level_index * slot_count, slot_count
    )
    received = lax.all_to_all(
        lax.all_to_all(arranged, "wave", split_axis=0, concat_axis=4, tiled=True),
        "lev",
        split_axis=0,
        concat_axis=3,
        tiled=True,
    )
    symmetric, antisymmetric = fold_rows(received, north_rows, south_rows, weight_row)
    tables = legendre_tables(orders, cosine_row, sine_row, wave_count, wave_count)
    updated = vertical(
        analyze(symmetric, antisymmetric, tables), orders, matrices, wave_count
    ).astype(jnp.bfloat16)
    gridded = unfold_rows(updated, tables, mirror_index, mirror_sign, inverse_scale)
    returned = lax.all_to_all(
        lax.all_to_all(gridded, "wave", split_axis=4, concat_axis=0, tiled=True),
        "lev",
        split_axis=3,
        concat_axis=0,
        tiled=True,
    )
    wave_part = slot_numbers // per_device
    remainder = slot_numbers % per_device
    source = (
        remainder // slot_count * (wave_devices * slot_count)
        + wave_part * slot_count
        + remainder % slot_count
    )
    spectral_state = lax.all_to_all(updated, "lev", split_axis=3, concat_axis=0, tiled=True)
    grid_field = jnp.transpose(jnp.take(returned, source, axis=0), (1, 2, 3, 4, 0))
    return (spectral_state, grid_field)


def solution(mesh):
    in_specs = (P(None, None, "lev", "wave", None), P(), P(), P(), P(), P(), P(), P())
    out_specs = (P("wave", None, None, "lev", None), P(None, None, "lev", "wave", None))
    return jax.shard_map(body, mesh=mesh, in_specs=in_specs, out_specs=out_specs, check_vma=False)
```

profile of v0, /device:TPU:1, one launch (start us, length us, event | category | flops | bytes accessed | tf_op | source)
XLA Modules:
  0.0 1388.9 jit_solution(10753938161685176272)
XLA Ops:
  2.1 4.5 copy.123
  6.6 9.3 gather_fusion
  15.9 6.3 broadcast_select_fusion
  22.2 4.1 reshape.4007
  26.3 16.3 %all-to-all-start = ((bf16[128,2,800]{2,1,0:T(2,128)(2,1)}), bf16[128,2,800]{2,1,0:T(2,128)(2,1)S(1)}, u32[]{:S(2)}, u32[]{:S(2)}) async-start(bf16[128,2,800]{2,1,0:T(2,128)(2,1)} %reshape.4007), calls=%async_computation | async-start | bytes 917504 | tf_op jit(solution)/shard_map/all_to_all | solution.py:178
  43.7 10.2 scatter_custom_fusion
  54.2 962.8 %while.23 = (s32[]{:T(128)}, f32[5,1280]{1,0:T(8,128)S(1)}, f32[5,1280]{1,0:T(8,128)S(1)}, f32[5,1280]{1,0:T(8,128)S(1)}, bf16[20,32,5,1280]{3,2,1,0:T(8,128)(2,...) while((s32[]{:T(128)}, f32[5,1280]{1,0:T(8,128)S(1)}, ...), condition=%wide.region_2.4_spmd.clone.clone, body=%wide.region_1.0_spmd.clone.clone.sunk | while | flops 3783808 | bytes 10983943 | solution.py:56
  101.1 1.2 bitcast_dynamic-update-slice_fusion.3
  149.3 1.2 bitcast_dynamic-update-slice_fusion.3
  197.5 1.2 bitcast_dynamic-update-slice_fusion.3
  293.7 1.2 bitcast_dynamic-update-slice_fusion.3
  341.8 1.2 bitcast_dynamic-update-slice_fusion.3
  390.0 1.2 bitcast_dynamic-update-slice_fusion.3
  438.1 1.2 bitcast_dynamic-update-slice_fusion.3
  486.2 1.2 bitcast_dynamic-update-slice_fusion.3
  534.4 1.2 bitcast_dynamic-update-slice_fusion.3
  582.5 1.1 bitcast_dynamic-update-slice_fusion.3
  630.6 1.2 bitcast_dynamic-update-slice_fusion.3
  678.8 1.3 bitcast_dynamic-update-slice_fusion.3
  775.1 1.1 bitcast_dynamic-update-slice_fusion.3
  823.2 1.2 bitcast_dynamic-update-slice_fusion.3
  919.5 1.2 bitcast_dynamic-update-slice_fusion.3
  967.7 1.2 bitcast_dynamic-update-slice_fusion.3
  1015.8 1.2 bitcast_dynamic-update-slice_fusion.3
  1017.2 2.5 reshape.4008
  1019.7 2.2 copy.124
  1021.9 6.6 all_to_all.68
  1028.6 5.1 all_to_all.90
  1034.0 11.6 copy.126
  1045.6 13.5 gather_fusion.2
  1059.1 6.8 copy.127
  1065.9 13.5 gather_fusion.3
  1079.4 6.9 copy.129
  1086.3 7.4 fusion.533
  1093.7 7.4 fusion.530
  1101.3 10.7 copy.132
  1112.0 9.0 fusion.581
  1121.1 3.3 copy.172
  1124.4 3.3 copy.171
  1130.7 5.0 slice.27
  1135.7 5.0 slice.26
  1140.8 3.8 all-to-all-start.2
  1144.6 7.1 fusion.515
  1151.7 6.8 copy.143
  1158.5 22.3 %gather_fusion.5 = f32[2560,5,2,2,4]{1,4,3,2,0:T(4,128)} fusion(f32[5,2,2,4,1280]{0,3,4,2,1:T(4,128)} %copy.143, s32[3072]{0:T(1024)S(1)} %pad_clamp_fusion), kind=kCustom, calls=%fused_computation.3.clone | custom fusion | bytes 1648640 | tf_op jit(solution)/shard_map/jit(_take)/gather | solution.py:127
  1180.8 14.9 %copy.144 = f32[2560,5,2,2,4]{0,4,3,2,1:T(4,128)S(1)} copy(f32[2560,5,2,2,4]{1,4,3,2,0:T(4,128)} %gather_fusion.5) | data formatting | bytes 1638400 | tf_op jit(solution)/shard_map/jit(_take)/gather | solution.py:127
  1195.7 7.1 fusion.519
  1202.8 6.7 copy.139
  1209.5 22.3 %gather_fusion.4 = f32[2560,5,2,2,4]{1,4,3,2,0:T(4,128)} fusion(f32[5,2,2,4,1280]{0,3,4,2,1:T(4,128)} %copy.139, s32[3072]{0:T(1024)S(1)} %pad_clamp_fusion), kind=kCustom, calls=%fused_computation.1.clone | custom fusion | bytes 1648640 | tf_op jit(solution)/shard_map/jit(_take)/gather | solution.py:127
  1231.8 14.9 %copy.140 = f32[2560,5,2,2,4]{0,4,3,2,1:T(4,128)S(1)} copy(f32[2560,5,2,2,4]{1,4,3,2,0:T(4,128)} %gather_fusion.4) | data formatting | bytes 1638400 | tf_op jit(solution)/shard_map/jit(_take)/gather | solution.py:127
  1247.1 10.5 copy.145
  1257.6 16.6 %reshape.4009 = bf16[128,2,800]{2,1,0:T(2,128)(2,1)} reshape(bf16[2560,2,2,4,5]{4,3,2,1,0:T(4,128)(2,1)} %bitcast.2155) | data formatting | bytes 819200
  1274.2 13.5 all-to-all-start.3
  1287.6 5.2 scatter_custom_fusion.1
  1293.8 11.7 all-to-all-done.3
  1305.5 23.6 %reshape.4010 = bf16[2560,2,2,4,5]{4,3,2,1,0:T(4,128)(2,1)} reshape(bf16[128,2,800]{2,1,0:T(2,128)(2,1)S(1)} %all-to-all-done.3) | data formatting | bytes 819200
  1329.1 19.5 %copy.168 = bf16[5,2,2,4,128,20]{5,4,3,2,1,0:T(8,128)(2,1)} copy(bf16[5,2,2,4,128,20]{0,3,2,1,5,4:T(4,128)(2,1)} %bitcast.2156) | data formatting | bytes 819200 | tf_op jit(solution)/shard_map/all_to_all | solution.py:191
  1348.6 3.8 copy.147
  1352.4 2.5 copy.148
  1354.9 6.1 all_to_all.91
  1361.1 4.9 copy.169
  1366.0 10.8 gather_fusion.1
  1376.8 5.7 fusion.523
  1382.5 6.3 copy.151
  (1100 shorter events, 118.0 us)
Async XLA Ops:
  0.6 1127.1 %copy-start = (f32[4,4]{1,0:T(4,128)S(1)}, f32[4,4]{1,0:T(4,128)}, u32[]{:S(2)}) copy-start(f32[4,4]{1,0:T(4,128)} %param.17) | copy-start | bytes 196
  0.6 43.0 %copy-start.2 = (s32[2560]{0:T(1024)S(1)}, s32[2560]{0:T(1024)}, u32[]{:S(2)}) copy-start(s32[2560]{0:T(1024)} %param.15) | copy-start | bytes 30724
  26.3 990.9 %all-to-all-start = ((bf16[128,2,800]{2,1,0:T(2,128)(2,1)}), bf16[128,2,800]{2,1,0:T(2,128)(2,1)S(1)}, u32[]{:S(2)}, u32[]{:S(2)}) async-start(bf16[128,2,800]{2,1,0:T(2,128)(2,1)} %reshape.4007), calls=%async_computation | async-start | bytes 917504 | tf_op jit(solution)/shard_map/all_to_all | solution.py:178
  54.2 962.9 %copy-start.5 = (f32[4]{0:T(128)S(1)}, f32[4]{0:T(128)}, u32[]{:S(2)}) copy-start(f32[4]{0:T(128)} %param.18) | copy-start | bytes 52
  1121.1 7.2 copy-start.6
  1121.1 7.7 copy-start.3
  1121.1 8.2 copy-start.4
  1140.8 133.4 %all-to-all-start.2 = ((bf16[5,2,2,4,1280]{4,1,0,2,3:T(2,128)(2,1)}), bf16[5,2,2,4,1280]{4,1,0,2,3:T(2,128)(2,1)S(1)}, u32[]{:S(2)}, u32[]{:S(2)}) async-start(bf16[5,2,2,4,1280]{4,1,0,2,3:T(2,128)(2,1)} %copy.135), calls=%async_computation.2 | async-start | bytes 409600 | tf_op jit(solution)/shard_map/all_to_all | solution.py:204
  1274.2 31.4 %all-to-all-start.3 = ((bf16[128,2,800]{2,1,0:T(2,128)(2,1)}), bf16[128,2,800]{2,1,0:T(2,128)(2,1)S(1)}, u32[]{:S(2)}, u32[]{:S(2)}) async-start(bf16[128,2,800]{2,1,0:T(2,128)(2,1)} %reshape.4009), calls=%async_computation.3 | async-start | bytes 917504 | tf_op jit(solution)/shard_map/all_to_all | solution.py:191
  1361.1 27.7 %copy-start.1 = (f32[4,4]{1,0:T(4,128)S(1)}, f32[4,4]{1,0:T(4,128)}, u32[]{:S(2)}) copy-start(f32[4,4]{1,0:T(4,128)} %param.17) | copy-start | bytes 196
where the time goes:
time: 1410 us; the launch traced here: 1390 us
  loops' own time  832 us (59%)
  local copies, waits for them, and re-layouts  357 us (25%)
  other arithmetic  111 us (8%)
  starting transfers between devices  33.6 us (2%)
  matrix products  31 us (2%)
    another operation x1, loops' own time, legendre_tables(): lax.scan(block_step, (former, current, log_scale), block_starts)  832 us
    while x780, other arithmetic  74.3 us
    unnamed x22, local copies, waits for them, and re-layouts  64.2 us
    gather x2, local copies, waits for them, and re-layouts, unfold_rows(): jnp.take(folded_sym, mirror_index, axis=4)  37.2 us
    gather x2, local copies, waits for them, and re-layouts, unfold_rows(): jnp.take(folded_anti, mirror_index, axis=4)  37.2 us
  transfers between devices with their start and end apart: 3, of which 1 were waited for; matrix products, arithmetic and copies ran while one was open for 20% of the time, Pallas kernels for 0%

commit v1 on v0

v1 whole, which is shorter than its diff:
```python
import functools
import math

import jax
import jax.numpy as jnp
import numpy as np
from jax import lax
from jax.experimental import pallas as pl
from jax.experimental.pallas import tpu as pltpu
from jax.sharding import PartitionSpec as P

MESH = pl.DeviceIdType.MESH
F32 = jnp.float32
BF16 = jnp.bfloat16

WAVES = 1280
NLAT = 2560
HEMI = NLAT // 2
NW = 128
ROWS = NLAT // NW
SLOTS = 5
TILES = HEMI // 128
CHAIN = 1296
BLOCKS = CHAIN // 16
PAD = 1408
ORDER = ((0, 1, 2, 3, 4), (6, 7, 8, 9, 5))
VMEM = 60 * 1024 * 1024


def constants():
    colat = np.pi * (np.arange(HEMI) + 0.5) / NLAT
    mixed = np.array(list(range(8)) + [8, 9] * 4)
    cosine = np.cos(colat).reshape(TILES, 128)[mixed].astype(np.float32)
    logsin = np.log(np.sin(colat)).reshape(TILES, 128)[mixed].astype(np.float32)
    weight = (math.sqrt(math.pi / NLAT) * np.sin(colat)).reshape(TILES, 128).T.astype(np.float32)
    start = np.array(
        [
            0.5 * (math.lgamma(m + 1.5) - math.lgamma(m + 1.0) - math.lgamma(1.5) - math.log(2.0))
            for m in range(WAVES)
        ],
        np.float32,
    )
    return cosine, logsin, weight, start


def iota(shape, axis):
    return lax.broadcasted_iota(jnp.int32, shape, axis)


def onehot(condition):
    return jnp.where(condition, 1.0, 0.0).astype(BF16)


def slot_onehot(core, slots_ref, hot):
    numbers = slots_ref[...]
    waves = iota((NW, WAVES), 1)
    for s in range(SLOTS):
        mine = jnp.where(
            core == 0,
            numbers[:, ORDER[0][s] : ORDER[0][s] + 1],
            numbers[:, ORDER[1][s] : ORDER[1][s] + 1],
        )
        hot[s * NW : (s + 1) * NW, :] = onehot(mine == waves)


def exchange(wave, core, send, land, own_sem, send_sem, recv_sem):
    own = pltpu.make_async_copy(send.at[wave], land.at[wave], own_sem)
    own.start()

    def start(step, _):
        target = lax.rem(wave + step, NW)
        pltpu.make_async_remote_copy(
            src_ref=send.at[target],
            dst_ref=land.at[wave],
            send_sem=send_sem,
            recv_sem=recv_sem,
            device_id=(target, core),
            device_id_type=MESH,
        ).start()
        return 0

    lax.fori_loop(1, NW, start, 0)

    def finish():
        own.wait()
        pltpu.make_async_copy(
            send.at[pl.ds(0, NW - 1)], land.at[pl.ds(0, NW - 1)], send_sem
        ).wait()
        pltpu.make_async_copy(
            send.at[pl.ds(0, NW - 1)], land.at[pl.ds(0, NW - 1)], recv_sem
        ).wait()

    return finish


def to_partner(wave, core, src, dst, send_sem, recv_sem):
    copy = pltpu.make_async_remote_copy(
        src_ref=src,
        dst_ref=dst,
        send_sem=send_sem,
        recv_sem=recv_sem,
        device_id=(wave, 1 - core),
        device_id_type=MESH,
    )
    copy.start()
    return copy


def forward_kernel(
    x_ref, slots_ref, out_ref, other, hot, rows, wide, send, land,
    pair_send, pair_recv, own_sem, send_sem, recv_sem,
):
    wave, core = lax.axis_index("wave"), lax.axis_index("lev")
    copy = to_partner(wave, core, x_ref, other, pair_send, pair_recv)
    slot_onehot(core, slots_ref, hot)
    copy.wait()
    for f in range(8):
        mine = x_ref[f].astype(F32)
        theirs = other[f].astype(F32)
        for v, value in (
            (0, jnp.where(core == 0, mine, theirs)),
            (1, jnp.where(core == 0, theirs, mine)),
        ):
            at = v * 64 + f * 8
            rows[at : at + 8, :] = value[0:8]
            rows[128 + at : 128 + at + 8, :] = value[8:16]
            rows[256 + at : 256 + at + 8, :] = jnp.concatenate(
                [value[16:20], jnp.zeros((4, WAVES), F32)], axis=0
            )
    arranged = lax.dot_general(
        hot[...],
        rows[...].astype(BF16),
        (((1,), (1,)), ((), ())),
        preferred_element_type=F32,
    )
    for c in range(3):
        for s in range(SLOTS):
            wide[pl.ds(c * 5 + s, NW, stride=16), :] = arranged[
                s * NW : (s + 1) * NW, c * 128 : (c + 1) * 128
            ]
    wide[pl.ds(15, NW, stride=16), :] = jnp.zeros((NW, 128), F32)
    send[...] = wide[...].astype(BF16).reshape(NW, 16, 128)
    exchange(wave, core, send, land, own_sem, send_sem, recv_sem)()
    out_ref[...] = land[...]


def transform_kernel(
    own_ref, start_ref, pressure_ref, depths_ref, modes_ref, project_ref, heat_ref,
    in_ref, lat_ref, cosine_ref, logsin_ref, weight_ref,
    out_ref, state_ref,
    coef_v, coef_s, table, block, wide, folded_in, folds, spec, turned, shuffle, grid, north_south,
    coef_sem,
):
    lane = iota((1, 128), 1)
    firsts = [own_ref[0], own_ref[2], own_ref[4]]
    seconds = [own_ref[1], own_ref[3], 0]
    begins = [(WAVES - firsts[c] + 15) // 16 * 16 for c in range(2)] + [CHAIN + 16]

    j = iota((8, PAD), 1)
    row = iota((8, PAD), 0)

    def per_chain(values):
        which = row % 4
        return jnp.where(which == 0, values[0], jnp.where(which == 1, values[1], values[2]))

    begin = per_chain(begins)
    second = j >= begin
    order = jnp.where(second, per_chain(seconds), per_chain(firsts))
    k = jnp.where(second, j - begin, j)
    n = (order + k).astype(F32)
    m = order.astype(F32)
    ok = (k >= 1) & (order + k < WAVES)
    grow = jnp.sqrt((4.0 * n * n - 1.0) / jnp.where(ok, n * n - m * m, 1.0))
    less = n - 1.0
    damp = jnp.sqrt(
        jnp.where(ok, jnp.maximum(less * less - m * m, 0.0), 0.0)
        / jnp.where(ok & (less > 0.0), 4.0 * less * less - 1.0, 1.0)
    )
    coef = jnp.where(ok, jnp.where(row < 4, grow, grow * damp), 0.0)
    coef_v[...] = coef
    coef_copy = pltpu.make_async_copy(coef_v, coef_s, coef_sem)
    coef_copy.start()

    source = iota((1, 1024), 1)
    source = (source % 128) // 16 * 128 + source % 16 * 8 + source // 128
    valid = iota((1, 1024), 1) % 128 < 80
    shuffle[...] = onehot(valid & (iota((640, 1024), 0) == source))
    wide[...] = in_ref[...].astype(F32).reshape(NW * 16, 128)
    lat = lat_ref[...]
    sign = jnp.where(lat < HEMI, 1.0, -1.0)
    for c in range(3):
        piece = jnp.concatenate(
            [wide[pl.ds(c * 5 + s, NW, stride=16), :].astype(BF16) for s in range(SLOTS)], axis=1
        )
        spread = jnp.dot(piece, shuffle[...], preferred_element_type=F32)
        for r in range(8 if c < 2 else 4):
            at = c * 8 + r
            part = spread[:, r * 128 : (r + 1) * 128]
            folded_in[at * NW : (at + 1) * NW, 0:128] = part.astype(BF16)
            folded_in[at * NW : (at + 1) * NW, 128:256] = (part * sign[:, at : at + 1]).astype(BF16)

    mirror = jnp.minimum(lat, NLAT - 1 - lat)
    mirror_rows = jnp.transpose(
        jnp.concatenate([mirror.astype(F32), jnp.zeros((NW, 128 - ROWS), F32)], axis=1)
    ).astype(jnp.int32)
    mirror_line = jnp.concatenate([mirror_rows[r : r + 1, :] for r in range(ROWS)], axis=1)

    def fold(t, _):
        hot = onehot(mirror_line == iota((256, NLAT), 0) + t * 256)
        total = jnp.dot(hot, folded_in[...], preferred_element_type=F32)
        at = pl.multiple_of(t * 256, 256)
        folds[pl.ds(at, 256), :] = total
        return 0

    lax.fori_loop(0, HEMI // 256, fold, 0)
    fold_total = [
        (folds[t * 128 : (t + 1) * 128, :] * weight_ref[:, t : t + 1]).astype(BF16)
        for t in range(TILES)
    ]
    for t in range(TILES):
        north_south[t * 128 : (t + 1) * 128, :] = fold_total[t]

    coef_copy.wait()
    cosine = [cosine_ref[0:8, :]] * 3 + [cosine_ref[8:16, :]]
    logsin = [logsin_ref[0:8, :]] * 3 + [logsin_ref[8:16, :]]
    sub = iota((8, 128), 0)

    def spread_rows(values):
        mixed = jnp.where(sub < 2, values[0], jnp.where(sub < 4, values[1], values[2]))
        return [values[0], values[1], values[2], mixed]

    def make(b, carry):
        current, former, scale = carry
        at_begin = [b * 16 == begins[c] for c in range(3)]
        wave_number = [
            jnp.where(at_begin[c], seconds[c], firsts[c]) for c in range(3)
        ]
        base = spread_rows([start_ref[w] for w in wave_number])
        degree = spread_rows([w.astype(F32) for w in wave_number])
        reset = spread_rows(
            [jnp.where((b == 0) | at_begin[c], 1.0, 0.0) for c in range(3)]
        )
        next_current, next_former, next_scale, factor = [], [], [], []
        for v in range(4):
            size = jnp.maximum(
                jnp.maximum(jnp.abs(current[v]), jnp.abs(former[v])), 1e-30
            )
            inverse = 1.0 / size
            again = reset[v] > 0.5
            if v < 3:
                again = jnp.broadcast_to(reset[v], (8, 128)) > 0.5
            next_current.append(jnp.where(again, 1.0, current[v] * inverse))
            next_former.append(jnp.where(again, 0.0, former[v] * inverse))
            next_scale.append(
                jnp.where(again, base[v] + degree[v] * logsin[v], scale[v] + jnp.log(size))
            )
            factor.append(jnp.exp(next_scale[v]))
        current, former = next_current, next_former
        for o in range(16):
            for v in range(4):
                block[o * 32 + v * 8 : o * 32 + v * 8 + 8, :] = current[v] * factor[v]
            at = b * 16 + o + 1
            grow = spread_rows([coef_s[c, at] for c in range(3)])
            damp = spread_rows([coef_s[4 + c, at] for c in range(3)])
            following = [
                (cosine[v] * grow[v]) * current[v] - damp[v] * former[v] for v in range(4)
            ]
            former, current = current, following
        at = pl.multiple_of(b * 16, 16)
        for c in range(3):
            for t in range(TILES):
                line = c * 8 + t if t < 8 else 24 + 2 * c + t - 8
                table[c, pl.ds(at, 16), t * 128 : (t + 1) * 128] = block[
                    pl.ds(line, 16, stride=32), :
                ].astype(BF16)
        return (tuple(current), tuple(former), tuple(next_scale))

    zeros = tuple(jnp.zeros((8, 128), F32) for _ in range(4))
    lax.fori_loop(0, BLOCKS, make, (zeros, zeros, zeros))

    chain_of = lane // 32

    def lanes(values):
        return jnp.where(chain_of == 0, values[0], jnp.where(chain_of == 1, values[1], values[2]))

    is_second = (lane // 16) % 2 == 1
    lane_begin = lanes(begins)
    offset = jnp.where(is_second, lanes(seconds) - lane_begin, lanes(firsts))
    level = (lane // 8) % 2 * 2 + lane % 2
    field = (lane // 2) % 2
    depth = jnp.zeros((1, 128), F32)
    for a in range(4):
        depth = jnp.where(level == a, depths_ref[a], depth)
    across, down = iota((128, 128), 1), iota((128, 128), 0)
    same = (across // 16 == down // 16) & ((across // 4) % 2 == (down // 4) % 2)
    level_to, level_from = (across // 8) % 2 * 2 + across % 2, (down // 8) % 2 * 2 + down % 2
    field_to, field_from = (across // 2) % 2, (down // 2) % 2

    def matrix(entry, to, of):
        total = jnp.zeros((128, 128), F32)
        for a in range(4):
            for b in range(4):
                total = jnp.where((level_to == a) & (level_from == b), entry(a, b), total)
        return jnp.where(same & (field_to == to) & (field_from == of), total, 0.0)

    def product(one, two):
        return lambda a, b: sum(one[a, e] * two[e, b] for e in range(4))

    first_matrix = jnp.concatenate(
        [
            matrix(lambda a, b: project_ref[a, b], 0, 0),
            matrix(product(project_ref, pressure_ref), 0, 1),
        ],
        axis=1,
    )
    second_matrix = matrix(lambda a, b: modes_ref[a, b], 0, 0) - matrix(
        product(heat_ref, modes_ref), 1, 0
    )
    turned[:, CHAIN - 16 : PAD] = jnp.zeros((128, PAD - CHAIN + 16), F32)
    spec[CHAIN - 16 : PAD, :] = jnp.zeros((PAD - CHAIN + 16, 128), F32)
    step_rows = CHAIN // 3

    def solve(q, _):
        at = pl.multiple_of(q * step_rows, 16)
        j = iota((step_rows, 128), 0) + at
        parts = []
        for c in range(3):
            both = jnp.dot(
                table[c, pl.ds(at, step_rows), :], north_south[...], preferred_element_type=F32
            )
            parts.append(jnp.where(j % 2 == 0, both[:, 0:128], both[:, 128:256]))
        spectrum = jnp.where(chain_of == 0, parts[0], jnp.where(chain_of == 1, parts[1], parts[2]))
        spectrum = jnp.where((j >= lane_begin) == is_second, spectrum, 0.0)
        n = (j + offset).astype(F32)
        coupling = n * (n + 1.0) * (1.0 / float(WAVES * WAVES))
        mixed = jnp.dot(
            spectrum, first_matrix, precision=lax.Precision.HIGHEST, preferred_element_type=F32
        )
        scaled = (mixed[:, 0:128] + coupling * mixed[:, 128:256]) / (1.0 + coupling * depth)
        updated = jnp.dot(
            scaled, second_matrix, precision=lax.Precision.HIGHEST, preferred_element_type=F32
        ) + jnp.where(field == 1, spectrum, 0.0)
        spec[pl.ds(at, step_rows), :] = updated.astype(BF16).astype(F32)
        return 0

    lax.fori_loop(0, 3, solve, 0)
    for t in range(PAD // 128):
        turned[:, t * 128 : (t + 1) * 128] = jnp.transpose(spec[t * 128 : (t + 1) * 128, :])
    for s in range(SLOTS):
        for v in range(2):
            value = turned[s * 16 + v * 8 : s * 16 + v * 8 + 8, :]
            if s % 2 == 1:
                value = pltpu.roll(value, PAD - begins[s // 2], 1)
            state_ref[v, s] = value[:, 0:WAVES].astype(BF16)

    even = iota((1, CHAIN), 1) % 2 == 0
    inverse_scale = 1.0 / math.sqrt(WAVES)
    for c in range(3):
        state = turned[c * 32 : c * 32 + 32, 0:CHAIN]
        left = jnp.concatenate(
            [jnp.where(even, state, 0.0), jnp.where(even, 0.0, state)], axis=0
        ).astype(BF16)
        for t in range(HEMI // 256):
            both = jnp.dot(
                left, table[c, :, t * 256 : (t + 1) * 256], preferred_element_type=F32
            )
            for u in range(2):
                sym = both[0:32, u * 128 : (u + 1) * 128]
                anti = both[32:64, u * 128 : (u + 1) * 128]
                at = t * 256 + u * 128
                wide[at : at + 128, c * 32 : c * 32 + 32] = jnp.transpose(
                    (sym + anti) * inverse_scale
                )
                folds[at : at + 128, c * 32 : c * 32 + 32] = jnp.transpose(
                    (sym - anti) * inverse_scale
                )
    used = lane < 80
    north_south[:, 0:128] = jnp.where(used, wide[0:HEMI, :], 0.0).astype(BF16)
    north_south[:, 128:256] = jnp.where(used, folds[:, 0:128], 0.0).astype(BF16)

    latitudes = iota((NW, HEMI), 1)
    for q in range(5):
        hot = jnp.concatenate(
            [onehot(mirror[:, r : r + 1] == latitudes) for r in range(q * 4, q * 4 + 4)], axis=0
        )
        both = jnp.dot(hot, north_south[...], preferred_element_type=F32)
        for u in range(4):
            r = q * 4 + u
            part = both[u * NW : (u + 1) * NW]
            grid[:, r * 128 : (r + 1) * 128] = jnp.where(
                sign[:, r : r + 1] > 0.0, part[:, 0:128], part[:, 128:256]
            ).astype(BF16)
    grid[:, ROWS * 128 : 24 * 128] = jnp.zeros((NW, 512), BF16)
    for c in range(3):
        piece = lax.dot_general(
            grid[:, c * 1024 : (c + 1) * 1024],
            shuffle[...],
            (((1,), (1,)), ((), ())),
            preferred_element_type=F32,
        )
        for s in range(SLOTS):
            wide[pl.ds(c * 5 + s, NW, stride=16), :] = piece[:, s * 128 : (s + 1) * 128]
    wide[pl.ds(15, NW, stride=16), :] = jnp.zeros((NW, 128), F32)
    out_ref[...] = wide[...].astype(BF16).reshape(NW, 16, 128)


def backward_kernel(
    in_ref, state_ref, slots_ref, spectral_ref, grid_ref,
    hot, wide, land, state_other, half, half_other,
    own_sem, send_sem, recv_sem, state_send, state_recv, pair_send, pair_recv,
):
    wave, core = lax.axis_index("wave"), lax.axis_index("lev")
    state_copy = to_partner(wave, core, state_ref.at[1 - core], state_other, state_send, state_recv)
    finish = exchange(wave, core, in_ref, land, own_sem, send_sem, recv_sem)
    slot_onehot(core, slots_ref, hot)
    state_copy.wait()
    for s in range(SLOTS):
        mine = jnp.where(core == 0, state_ref[0, s].astype(F32), state_ref[1, s].astype(F32))
        theirs = state_other[s].astype(F32)
        spectral_ref[ORDER[0][s]] = jnp.where(core == 0, mine, theirs).astype(BF16)
        spectral_ref[ORDER[1][s]] = jnp.where(core == 0, theirs, mine).astype(BF16)
    finish()
    wide[...] = land[...].astype(F32).reshape(NW * 16, 128)
    left = jnp.concatenate(
        [
            jnp.concatenate(
                [
                    jnp.transpose(wide[pl.ds(c * 5 + s, NW, stride=16), :])
                    for s in range(SLOTS)
                ],
                axis=1,
            )
            for c in range(3)
        ],
        axis=0,
    ).astype(BF16)
    rows = jnp.dot(left, hot[...], preferred_element_type=F32)
    kept = []
    for f in range(8):
        values = []
        for v in range(2):
            at = v * 64 + f * 8
            values.append(
                jnp.concatenate(
                    [rows[at : at + 8], rows[128 + at : 136 + at], rows[256 + at : 260 + at]],
                    axis=0,
                )
            )
        half[f] = jnp.where(core == 0, values[1], values[0]).astype(BF16)
        kept.append(jnp.where(core == 0, values[0], values[1]))
    copy = to_partner(wave, core, half, half_other, pair_send, pair_recv)
    copy.wait()
    for f in range(8):
        grid_ref[f] = (kept[f] + half_other[f].astype(F32)).astype(BF16)


def vmem():
    return pl.BlockSpec(memory_space=pltpu.VMEM)


def smem():
    return pl.BlockSpec(memory_space=pltpu.SMEM)


DMA = pltpu.SemaphoreType.DMA


def forward(x, slots):
    return pl.pallas_call(
        forward_kernel,
        out_shape=jax.ShapeDtypeStruct((NW, 16, 128), BF16),
        in_specs=[vmem(), vmem()],
        out_specs=vmem(),
        scratch_shapes=[
            pltpu.VMEM((8, ROWS, WAVES), BF16),
            pltpu.VMEM((SLOTS * NW, WAVES), BF16),
            pltpu.VMEM((384, WAVES), F32),
            pltpu.VMEM((NW * 16, 128), F32),
            pltpu.VMEM((NW, 16, 128), BF16),
            pltpu.VMEM((NW, 16, 128), BF16),
            DMA, DMA, DMA, DMA, DMA,
        ],
        compiler_params=pltpu.CompilerParams(vmem_limit_bytes=VMEM, has_side_effects=True),
    )(x, slots)


def transform(own, matrices, received, lat):
    cosine, logsin, weight, start = constants()
    pressure, depths, modes, project, heat = matrices
    return pl.pallas_call(
        transform_kernel,
        out_shape=(
            jax.ShapeDtypeStruct((NW, 16, 128), BF16),
            jax.ShapeDtypeStruct((2, SLOTS, 8, WAVES), BF16),
        ),
        in_specs=[smem()] * 7 + [vmem()] * 5,
        out_specs=(vmem(), vmem()),
        scratch_shapes=[
            pltpu.VMEM((8, PAD), F32),
            pltpu.SMEM((8, PAD), F32),
            pltpu.VMEM((3, CHAIN, HEMI), BF16),
            pltpu.VMEM((16 * 32, 128), F32),
            pltpu.VMEM((NW * 16, 128), F32),
            pltpu.VMEM((NLAT, 256), BF16),
            pltpu.VMEM((HEMI, 256), F32),
            pltpu.VMEM((PAD, 128), F32),
            pltpu.VMEM((128, PAD), F32),
            pltpu.VMEM((640, 1024), BF16),
            pltpu.VMEM((NW, 24 * 128), BF16),
            pltpu.VMEM((HEMI, 256), BF16),
            DMA,
        ],
        compiler_params=pltpu.CompilerParams(vmem_limit_bytes=VMEM),
    )(
        own, jnp.asarray(start), pressure, depths, modes, project, heat,
        received, lat, jnp.asarray(cosine), jnp.asarray(logsin), jnp.asarray(weight),
    )


def backward(blocks, state, slots):
    return pl.pallas_call(
        backward_kernel,
        out_shape=(
            jax.ShapeDtypeStruct((2 * SLOTS, 8, WAVES), BF16),
            jax.ShapeDtypeStruct((8, ROWS, WAVES), BF16),
        ),
        in_specs=[vmem(), vmem(), vmem()],
        out_specs=(vmem(), vmem()),
        scratch_shapes=[
            pltpu.VMEM((SLOTS * NW, WAVES), BF16),
            pltpu.VMEM((NW * 16, 128), F32),
            pltpu.VMEM((NW, 16, 128), BF16),
            pltpu.VMEM((SLOTS, 8, WAVES), BF16),
            pltpu.VMEM((8, ROWS, WAVES), BF16),
            pltpu.VMEM((8, ROWS, WAVES), BF16),
            DMA, DMA, DMA, DMA, DMA, DMA, DMA,
        ],
        compiler_params=pltpu.CompilerParams(vmem_limit_bytes=VMEM, has_side_effects=True),
    )(blocks, state, slots)


def body(
    fourier,
    lat_rows,
    wave_slots,
    pressure_balance_operator,
    depths,
    vertical_modes,
    mode_projection,
    heat_link_operator,
):
    wave, core = lax.axis_index("wave"), lax.axis_index("lev")
    slots = wave_slots.reshape(NW, 2 * SLOTS)
    lat = lat_rows.reshape(NW, ROWS)
    ten = lax.dynamic_slice_in_dim(wave_slots, wave * 2 * SLOTS, 2 * SLOTS)
    own = jnp.where(core == 0, ten[np.array(ORDER[0])], ten[np.array(ORDER[1])])
    matrices = (
        pressure_balance_operator, depths, vertical_modes, mode_projection, heat_link_operator,
    )
    received = forward(fourier.reshape(8, ROWS, WAVES), slots)
    blocks, state = transform(own, matrices, received, lat)
    spectral, grid = backward(blocks, state, slots)
    return (
        spectral.reshape(2 * SLOTS, 2, 2, 2, WAVES),
        grid.reshape(2, 2, 2, ROWS, WAVES),
    )


def solution(mesh):
    in_specs = (P(None, None, "lev", "wave", None), P(), P(), P(), P(), P(), P(), P())
    out_specs = (P("wave", None, None, "lev", None), P(None, None, "lev", "wave", None))
    return jax.shard_map(body, mesh=mesh, in_specs=in_specs, out_specs=out_specs, check_vma=False)
```

time: 1410 us -> 119 us (0.08); the launches traced: 1390 us -> 118 us
  loops' own time: 832 us -> 0 us
  local copies, waits for them, and re-layouts: 357 us -> 8.17 us
  other arithmetic: 111 us -> 0.56 us
  Pallas kernels: 0 us -> 109 us
  starting transfers between devices: 33.6 us -> 0 us
  matrix products: 31 us -> 0 us
    another operation x1 -> x0, loops' own time: 832 us -> none  [legendre_tables(): lax.scan(block_step, (former, current, log_scale), block_starts)]
    gather x10 -> x2, local copies, waits for them, and re-layouts: 135 us -> 1.29 us  [body(): own = jnp.where(core == 0, ten[np.array(ORDER[0])], ten[np.array(ORDER[1])])]
    pallas_call x0 -> x3, Pallas kernels: none -> 109 us  [the longest x1 38.2 us: transform(): pl.pallas_call(transform_kernel, out_shape=(jax.ShapeDtypeStruct((NW, 16,...]
    while x780 -> x0, other arithmetic: 74.3 us -> none
    unnamed x22 -> x10, local copies, waits for them, and re-layouts: 64.2 us -> 3.63 us
    all_to_all x9 -> x0, local copies, waits for them, and re-layouts: 52.3 us -> none  [the longest x3 25.8 us: body(): lax.all_to_all(gridded, 'wave', split_axis=4, concat_axis=0, tiled=True)]
    all_to_all x3 -> x0, starting transfers between devices: 33.6 us -> none  [the longest x1 16.3 us: body(): lax.all_to_all(arranged, 'wave', split_axis=0, concat_axis=4, tiled=True)]
    dot_general x8 -> x0, matrix products: 31 us -> none  [the longest x1 7.44 us: analyze(): jnp.einsum('mrfvh,kmh->mrfvk', symmetric, even_table, preferred_element_t...]
  transfers between devices with their start and end apart: 3 -> 0, of which waited for: 1 -> 0; matrix products, arithmetic and copies ran while one was open for 20% -> 0% of each run, Pallas kernels for 0% -> 0%
where the time goes in v1:
time: 119 us; the launch traced here: 118 us
  Pallas kernels  109 us (92%)
  local copies, waits for them, and re-layouts  8.17 us (7%)
    pallas_call x1, Pallas kernels, transform(): pl.pallas_call(transform_kernel, out_shape=(jax.ShapeDtypeStruct((NW, 16,...  38.2 us
    pallas_call x1, Pallas kernels, forward(): pl.pallas_call(forward_kernel, out_shape=jax.ShapeDtypeStruct((NW, 16, 12...  37.4 us
    pallas_call x1, Pallas kernels, backward(): pl.pallas_call(backward_kernel, out_shape=(jax.ShapeDtypeStruct((2 * SLOT...  33.1 us
    unnamed x10, local copies, waits for them, and re-layouts  3.63 us

profile of v1, /device:TPU:1, one launch (start us, length us, event | category | flops | bytes accessed | tf_op | source)
XLA Modules:
  0.0 118.1 jit_solution(14399750036083352111)
XLA Ops:
  0.6 0.0 copy-start.2
  0.6 0.7 copy-done.2
  1.3 0.1 dynamic_slice.3
  1.4 0.0 copy-start.3
  1.4 0.6 gather_fusion
  2.1 0.0 copy-done.3
  2.1 0.0 copy-start
  2.1 0.6 gather_fusion.1
  2.7 0.5 broadcast_select_fusion.own_ref
  3.3 0.0 copy-start.1
  3.3 0.8 reshape.20.slots_ref
  4.1 0.0 copy-done.1
  4.1 0.7 reshape.21.lat_ref
  4.8 0.0 copy-done
  4.8 0.8 copy.20
  5.6 37.4 %shard_map.167.in_ref = bf16[128,16,128]{2,1,0:T(8,128)(2,1)} custom-call(bf16[8,20,1280]{2,1,0:T(8,128)(2,1)} %bitcast.2, s32[128,10]{1,0:T(8,128)} %reshape.20.slots_ref), custom_call_target="tpu_custom_call" | custom-call | tf_op jit(solution)/shard_map/pallas_call | solution.py:469
  43.0 38.2 %shard_map.168 = (bf16[128,16,128]{2,1,0:T(8,128)(2,1)}, bf16[2,5,8,1280]{3,2,1,0:T(8,128)(2,1)}) custom-call(s32[5]{0:T(128)} %broadcast_select_fusion.own_ref, f32[1280]{0:T(1024)} %constant.33.clone.start_ref, f32[4,4]{1,0:T(4,128)} %pressure_ref.1, f32[4]{0:T(128)} %depths_ref.1, f32[4,4]{1,0:T(4,128)} %modes_ref.1, f32[4,4]{1,0:T(4,128)} %project_ref.1, ...), custom_call_target="tpu_custom_call" | custom-call | tf_op jit(solution)/shard_map/pallas_call | solution.py:490
  81.3 33.1 %shard_map.169 = (bf16[10,8,1280]{2,1,0:T(8,128)(2,1)}, bf16[8,20,1280]{2,1,0:T(8,128)(2,1)}) custom-call(bf16[128,16,128]{2,1,0:T(8,128)(2,1)} %get-tuple-element.6.in_ref, bf16[2,5,8,1280]{3,2,1,0:T(8,128)(2,1)} %get-tuple-element.7.state_ref, s32[128,10]{1,0:T(8,128)} %reshape.20.slots_ref), custom_call_target="tpu_custom_call" | custom-call | tf_op jit(solution)/shard_map/pallas_call | solution.py:521
  114.3 1.7 %reshape.22 = bf16[10,2,2,2,1280]{4,3,2,1,0:T(2,128)(2,1)} reshape(bf16[10,8,1280]{2,1,0:T(8,128)(2,1)} %get-tuple-element.8) | data formatting | bytes 409600 | tf_op jit(solution)/shard_map/reshape | solution.py:564
  116.0 2.1 %copy.21 = bf16[2,2,2,20,1280]{4,2,3,1,0:T(2,128)(2,1)} copy(bf16[2,2,2,20,1280]{4,3,2,1,0:T(8,128)(2,1)} %bitcast.3) | data formatting | bytes 819200
  (3 shorter events, 0.0 us)
Async XLA Ops:
  0.6 0.7 copy-start.2
  1.4 0.7 copy-start.3
  2.1 2.7 %copy-start = (bf16[2,2,2,20,1280]{4,2,3,1,0:T(2,128)(2,1)S(1)}, bf16[2,2,2,20,1280]{4,2,3,1,0:T(2,128)(2,1)}, u32[]{:S(2)}) copy-start(bf16[2,2,2,20,1280]{4,2,3,1,0:T(2,128)(2,1)} %param.16) | copy-start | bytes 1228804
  3.3 0.8 copy-start.1

commit v2 on v1

v2 whole, which is shorter than its diff:
```python
import functools
import math

import jax
import jax.numpy as jnp
import numpy as np
from jax import lax
from jax.experimental import pallas as pl
from jax.experimental.pallas import tpu as pltpu
from jax.sharding import PartitionSpec as P

MESH = pl.DeviceIdType.MESH
F32 = jnp.float32
BF16 = jnp.bfloat16

WAVES = 1280
NLAT = 2560
HEMI = NLAT // 2
NW = 128
ROWS = NLAT // NW
SLOTS = 5
TILES = HEMI // 128
CHAIN = 1296
BLOCKS = CHAIN // 16
PAD = 1408
ORDER = ((0, 1, 2, 3, 4), (6, 7, 8, 9, 5))
EARLY = 14
VMEM = 60 * 1024 * 1024
STRIDE = 17


def constants():
    colat = np.pi * (np.arange(HEMI) + 0.5) / NLAT
    mixed = np.array(list(range(8)) + [8, 9] * 4)
    cosine = np.cos(colat).reshape(TILES, 128)[mixed].astype(np.float32)
    logsin = np.log(np.sin(colat)).reshape(TILES, 128)[mixed].astype(np.float32)
    weight = (math.sqrt(math.pi / NLAT) * np.sin(colat)).reshape(TILES, 128).T.astype(np.float32)
    start = np.array(
        [
            0.5 * (math.lgamma(m + 1.5) - math.lgamma(m + 1.0) - math.lgamma(1.5) - math.log(2.0))
            for m in range(WAVES)
        ],
        np.float32,
    )
    return cosine, logsin, weight, start


def iota(shape, axis):
    return lax.broadcasted_iota(jnp.int32, shape, axis)


def onehot(condition):
    return jnp.where(condition, 1.0, 0.0).astype(BF16)


def slot_onehot(core, slots_ref, hot):
    numbers = slots_ref[...]
    waves = iota((NW, WAVES), 1)
    for s in range(SLOTS):
        mine = jnp.where(
            core == 0,
            numbers[:, ORDER[0][s] : ORDER[0][s] + 1],
            numbers[:, ORDER[1][s] : ORDER[1][s] + 1],
        )
        hot[s * NW : (s + 1) * NW, :] = onehot(mine == waves)


def remote(src, dst, send_sem, recv_sem, device):
    return pltpu.make_async_remote_copy(
        src_ref=src, dst_ref=dst, send_sem=send_sem, recv_sem=recv_sem,
        device_id=device, device_id_type=MESH,
    )


def split(value):
    high = value.astype(BF16)
    return high, (value - high.astype(F32)).astype(BF16)


def product_of_parts(value, high, low):
    one, two = split(value)
    return jnp.dot(
        jnp.concatenate([one, two], axis=1),
        jnp.concatenate([high, high], axis=0),
        preferred_element_type=F32,
    ) + jnp.dot(one, low, preferred_element_type=F32)


def kernel(
    waves_ref, start_ref, pressure_ref, depths_ref, modes_ref, project_ref, heat_ref,
    x_ref, slots_ref, lat_ref, cosine_ref, logsin_ref, weight_ref,
    grid_mine_ref, grid_other_ref, state_mine_ref, state_other_ref,
    other, hot, rows, wide, send, land, send_back, land_back,
    coef_v, coef_s, table, block, folded_in, folds, spec, turned, shuffle, north_south,
    ns_rows, mirror_ref, sign_ref, small, state_half, state_land, left, half, half_land,
    round_two, coef_sem, pair_send, pair_recv, own_sem, send_sem, recv_sem,
    state_send, state_recv, own_back_sem, send_back_sem, recv_back_sem, half_send, half_recv,
):
    wave, core = lax.axis_index("wave"), lax.axis_index("lev")
    partner = (wave, 1 - core)
    lane = iota((1, 128), 1)

    depth_at, plane_at = lax.div(wave, 16), lax.rem(wave, 16)
    barrier = pltpu.get_barrier_semaphore()

    def greet_depth(i, _):
        there = lax.rem(depth_at + i, 8) * 16 + plane_at
        pl.semaphore_signal(barrier, inc=1, device_id=(there, core), device_id_type=MESH)
        return 0

    def in_plane(i):
        return depth_at * 16 + lax.rem(plane_at + i, 16)

    def greet_plane(i, _):
        pl.semaphore_signal(barrier, inc=1, device_id=(in_plane(i), core), device_id_type=MESH)
        return 0

    def pass_on(i, _):
        pl.semaphore_signal(round_two, inc=1, device_id=(in_plane(i), core), device_id_type=MESH)
        return 0

    pl.semaphore_signal(barrier, inc=1, device_id=partner, device_id_type=MESH)
    lax.fori_loop(1, 8, greet_depth, 0)
    lax.fori_loop(1, 16, greet_plane, 0)

    held = [
        jnp.where(
            core == 0,
            waves_ref[wave * 2 * SLOTS + ORDER[0][s]],
            waves_ref[wave * 2 * SLOTS + ORDER[1][s]],
        )
        for s in range(SLOTS)
    ]
    firsts = [held[0], held[2], held[4]]
    seconds = [held[1], held[3], 0]
    begins = [(WAVES - firsts[c] + 15) // 16 * 16 for c in range(2)] + [CHAIN + 16]

    j = iota((8, PAD), 1)
    row = iota((8, PAD), 0)

    def per_chain(values):
        which = row % 4
        return jnp.where(which == 0, values[0], jnp.where(which == 1, values[1], values[2]))

    begin = per_chain(begins)
    second = j >= begin
    order = jnp.where(second, per_chain(seconds), per_chain(firsts))
    k = jnp.where(second, j - begin, j)
    n = (order + k).astype(F32)
    m = order.astype(F32)
    ok = (k >= 1) & (order + k < WAVES)
    grow = jnp.sqrt((4.0 * n * n - 1.0) / jnp.where(ok, n * n - m * m, 1.0))
    less = n - 1.0
    damp = jnp.sqrt(
        jnp.where(ok, jnp.maximum(less * less - m * m, 0.0), 0.0)
        / jnp.where(ok & (less > 0.0), 4.0 * less * less - 1.0, 1.0)
    )
    coef = jnp.where(ok, jnp.where(row < 4, grow, grow * damp), 0.0)
    coef_v[...] = coef
    coef_copy = pltpu.make_async_copy(coef_v, coef_s, coef_sem)
    coef_copy.start()

    slot_onehot(core, slots_ref, hot)

    pl.semaphore_wait(barrier, 7 + 15 + 1)
    lax.fori_loop(1, 16, pass_on, 0)
    pair = remote(x_ref, other, pair_send, pair_recv, partner)
    pair.start()

    source = iota((1, 1024), 1)
    source = (source % 128) // 16 * 128 + source % 16 * 8 + source // 128
    valid = iota((1, 1024), 1) % 128 < 80
    shuffle[...] = onehot(valid & (iota((640, 1024), 0) == source))

    def place(ref, side):
        for f in range(8):
            value = ref[f].astype(F32)
            at = pl.multiple_of(side * 64 + f * 8, 8)
            rows[0, pl.ds(at, 8), :] = value[0:8]
            rows[1, pl.ds(at, 8), :] = value[8:16]
            rows[2, pl.ds(at, 8), :] = jnp.concatenate(
                [value[16:20], jnp.zeros((4, WAVES), F32)], axis=0
            )

    place(x_ref, core)

    cosine = [cosine_ref[0:8, :]] * 3 + [cosine_ref[8:16, :]]
    logsin = [logsin_ref[0:8, :]] * 3 + [logsin_ref[8:16, :]]
    sub = iota((8, 128), 0)

    def spread_rows(values):
        mixed = jnp.where(sub < 2, values[0], jnp.where(sub < 4, values[1], values[2]))
        return [values[0], values[1], values[2], mixed]

    def make(b, carry):
        current, former, scale = carry
        at_begin = [b * 16 == begins[c] for c in range(3)]
        wave_number = [
            jnp.where(at_begin[c], seconds[c], firsts[c]) for c in range(3)
        ]
        base = spread_rows([start_ref[w] for w in wave_number])
        degree = spread_rows([w.astype(F32) for w in wave_number])
        reset = spread_rows(
            [jnp.where((b == 0) | at_begin[c], 1.0, 0.0) for c in range(3)]
        )
        next_current, next_former, next_scale, factor = [], [], [], []
        for v in range(4):
            size = jnp.maximum(
                jnp.maximum(jnp.abs(current[v]), jnp.abs(former[v])), 1e-30
            )
            inverse = 1.0 / size
            again = reset[v] > 0.5
            if v < 3:
                again = jnp.broadcast_to(reset[v], (8, 128)) > 0.5
            next_current.append(jnp.where(again, 1.0, current[v] * inverse))
            next_former.append(jnp.where(again, 0.0, former[v] * inverse))
            next_scale.append(
                jnp.where(again, base[v] + degree[v] * logsin[v], scale[v] + jnp.log(size))
            )
            factor.append(jnp.exp(next_scale[v]))
        current, former = next_current, next_former
        for o in range(16):
            for v in range(4):
                block[pl.ds(v * 8 * STRIDE + o, 8, stride=STRIDE), :] = current[v] * factor[v]
            at = b * 16 + o + 1
            grow = spread_rows([coef_s[c, at] for c in range(3)])
            damp = spread_rows([coef_s[4 + c, at] for c in range(3)])
            following = [
                (cosine[v] * grow[v]) * current[v] - damp[v] * former[v] for v in range(4)
            ]
            former, current = current, following
        at = pl.multiple_of(b * 16, 16)
        for c in range(3):
            for t in range(TILES):
                line = c * 8 + t if t < 8 else 24 + 2 * c + t - 8
                table[c, pl.ds(at, 16), t * 128 : (t + 1) * 128] = block[
                    line * STRIDE : line * STRIDE + 16, :
                ].astype(BF16)
        return (tuple(current), tuple(former), tuple(next_scale))

    coef_copy.wait()
    zeros = tuple(jnp.zeros((8, 128), F32) for _ in range(4))
    carry = lax.fori_loop(0, EARLY, make, (zeros, zeros, zeros))

    pair.wait()
    place(other, 1 - core)
    wide[pl.ds(15, NW, stride=STRIDE), :] = jnp.zeros((NW, 128), F32)
    for c in range(3):
        arranged = lax.dot_general(
            hot[...], rows[c].astype(BF16), (((1,), (1,)), ((), ())), preferred_element_type=F32
        )
        for s in range(SLOTS):
            wide[pl.ds(c * 5 + s, NW, stride=STRIDE), :] = arranged[s * NW : (s + 1) * NW]
    for w in range(NW):
        send[w] = wide[w * STRIDE : w * STRIDE + 16, :].astype(BF16)
    pl.semaphore_wait(round_two, 15)
    own = pltpu.make_async_copy(send.at[wave], land.at[wave], own_sem)
    own.start()

    def send_to(step):
        target = lax.rem(wave + step, NW)
        remote(send.at[target], land.at[wave], send_sem, recv_sem, (target, core)).start()

    def make_and_send(i, carry):
        send_to(2 * i + 1)
        send_to(2 * i + 2)
        return make(EARLY + i, carry)

    carry = lax.fori_loop(0, NW // 2 - 1, make_and_send, carry)
    send_to(NW - 1)
    lax.fori_loop(EARLY + NW // 2 - 1, BLOCKS, make, carry)

    lat = lat_ref[...]
    sign = jnp.where(lat < HEMI, 1.0, -1.0)
    mirror = jnp.minimum(lat, NLAT - 1 - lat)
    mirror_rows = jnp.transpose(
        jnp.concatenate([mirror.astype(F32), jnp.zeros((NW, 128 - ROWS), F32)], axis=1)
    ).astype(jnp.int32)
    mirror_line = jnp.concatenate([mirror_rows[r : r + 1, :] for r in range(ROWS)], axis=1)

    mirror_ref[...] = mirror
    sign_ref[...] = sign

    own.wait()
    all_but_one = pl.ds(0, NW - 1)
    pltpu.make_async_copy(send.at[all_but_one], land.at[all_but_one], send_sem).wait()
    pltpu.make_async_copy(send.at[all_but_one], land.at[all_but_one], recv_sem).wait()

    for w in range(NW):
        wide[w * STRIDE : w * STRIDE + 16, :] = land[w].astype(F32)
    for c in range(3):
        piece = jnp.concatenate(
            [wide[pl.ds(c * 5 + s, NW, stride=STRIDE), :].astype(BF16) for s in range(SLOTS)],
            axis=1,
        )
        spread = jnp.dot(piece, shuffle[...], preferred_element_type=F32)
        for r in range(8 if c < 2 else 4):
            at = c * 8 + r
            part = spread[:, r * 128 : (r + 1) * 128]
            folded_in[at * NW : (at + 1) * NW, 0:128] = part.astype(BF16)
            folded_in[at * NW : (at + 1) * NW, 128:256] = (part * sign[:, at : at + 1]).astype(BF16)

    def fold(t, _):
        hot = onehot(mirror_line == iota((256, NLAT), 0) + t * 256)
        total = jnp.dot(hot, folded_in[...], preferred_element_type=F32)
        at = pl.multiple_of(t * 256, 256)
        folds[pl.ds(at, 256), :] = total
        return 0

    lax.fori_loop(0, HEMI // 256, fold, 0)
    for t in range(TILES):
        north_south[t * 128 : (t + 1) * 128, :] = (
            folds[t * 128 : (t + 1) * 128, :] * weight_ref[:, t : t + 1]
        ).astype(BF16)

    chain_of = lane // 32

    def lanes(values):
        return jnp.where(chain_of == 0, values[0], jnp.where(chain_of == 1, values[1], values[2]))

    is_second = (lane // 16) % 2 == 1
    lane_begin = lanes(begins)
    offset = jnp.where(is_second, lanes(seconds) - lane_begin, lanes(firsts))
    level = (lane // 8) % 2 * 2 + lane % 2
    field = (lane // 2) % 2
    depth = jnp.zeros((1, 128), F32)
    for a in range(4):
        depth = jnp.where(level == a, depths_ref[a], depth)
    across, down = iota((128, 128), 1), iota((128, 128), 0)
    same = (across // 16 == down // 16) & ((across // 4) % 2 == (down // 4) % 2)
    level_to, level_from = (across // 8) % 2 * 2 + across % 2, (down // 8) % 2 * 2 + down % 2
    field_to, field_from = (across // 2) % 2, (down // 2) % 2

    def matrix(entry, to, of):
        total = jnp.zeros((128, 128), F32)
        for a in range(4):
            for b in range(4):
                total = jnp.where((level_to == a) & (level_from == b), entry(a, b), total)
        return jnp.where(same & (field_to == to) & (field_from == of), total, 0.0)

    def product(one, two):
        return lambda a, b: sum(one[a, e] * two[e, b] for e in range(4))

    first_matrix = jnp.concatenate(
        [
            matrix(lambda a, b: project_ref[a, b], 0, 0),
            matrix(product(project_ref, pressure_ref), 0, 1),
        ],
        axis=1,
    )
    second_matrix = matrix(lambda a, b: modes_ref[a, b], 0, 0) - matrix(
        product(heat_ref, modes_ref), 1, 0
    )
    first_parts, second_parts = split(first_matrix), split(second_matrix)
    turned[:, CHAIN - 16 : PAD] = jnp.zeros((128, PAD - CHAIN + 16), F32)
    spec[CHAIN - 16 : PAD, :] = jnp.zeros((PAD - CHAIN + 16, 128), F32)
    step_rows = CHAIN // 3

    def solve(q, _):
        at = pl.multiple_of(q * step_rows, 16)
        j = iota((step_rows, 128), 0) + at
        parts = []
        for c in range(3):
            both = jnp.dot(
                table[c, pl.ds(at, step_rows), :], north_south[...], preferred_element_type=F32
            )
            parts.append(jnp.where(j % 2 == 0, both[:, 0:128], both[:, 128:256]))
        spectrum = jnp.where(chain_of == 0, parts[0], jnp.where(chain_of == 1, parts[1], parts[2]))
        spectrum = jnp.where((j >= lane_begin) == is_second, spectrum, 0.0)
        n = (j + offset).astype(F32)
        coupling = n * (n + 1.0) * (1.0 / float(WAVES * WAVES))
        mixed = product_of_parts(spectrum, *first_parts)
        scaled = (mixed[:, 0:128] + coupling * mixed[:, 128:256]) / (1.0 + coupling * depth)
        updated = product_of_parts(scaled, *second_parts) + jnp.where(field == 1, spectrum, 0.0)
        spec[pl.ds(at, step_rows), :] = updated.astype(BF16).astype(F32)
        return 0

    lax.fori_loop(0, 3, solve, 0)
    for t in range(PAD // 128):
        turned[:, t * 128 : (t + 1) * 128] = jnp.transpose(spec[t * 128 : (t + 1) * 128, :])
    for s in range(SLOTS):
        for v in range(2):
            value = turned[s * 16 + v * 8 : s * 16 + v * 8 + 8, :]
            if s % 2 == 1:
                for bit in range(4, 11):
                    moved = pltpu.roll(value, PAD - (1 << bit) % PAD, 1)
                    value = jnp.where((begins[s // 2] >> bit) % 2 == 1, moved, value)
            state_half[v, s] = value[:, 0:WAVES].astype(BF16)
    state_copy = remote(
        state_half.at[1 - core], state_land, state_send, state_recv, partner
    )
    state_copy.start()

    even = iota((1, CHAIN), 1) % 2 == 0
    inverse_scale = 1.0 / math.sqrt(WAVES)
    ns_rows[:, 96:128, :] = jnp.zeros((2, 32, HEMI), F32)
    for c in range(3):
        state = turned[c * 32 : c * 32 + 32, 0:CHAIN]
        both_parities = jnp.concatenate(
            [jnp.where(even, state, 0.0), jnp.where(even, 0.0, state)], axis=0
        ).astype(BF16)
        for t in range(HEMI // 256):
            both = jnp.dot(
                both_parities, table[c, :, t * 256 : (t + 1) * 256], preferred_element_type=F32
            )
            sym, anti = both[0:32], both[32:64]
            ns_rows[0, c * 32 : c * 32 + 32, t * 256 : (t + 1) * 256] = (sym + anti) * inverse_scale
            ns_rows[1, c * 32 : c * 32 + 32, t * 256 : (t + 1) * 256] = (sym - anti) * inverse_scale
    for u in range(2):
        for t in range(TILES):
            north_south[t * 128 : (t + 1) * 128, u * 128 : (u + 1) * 128] = jnp.transpose(
                ns_rows[u, :, t * 128 : (t + 1) * 128]
            ).astype(BF16)

    latitudes = iota((32, HEMI), 1)
    small[pl.ds(15, 32, stride=STRIDE), :] = jnp.zeros((32, 128), F32)
    own_back = pltpu.make_async_copy(send_back.at[wave], land_back.at[wave], own_back_sem)
    for g in range(4):
        base = pl.multiple_of(lax.rem(lax.div(wave, 32) + g, 4) * 32, 32)
        near = mirror_ref[pl.ds(base, 32), :]
        side = sign_ref[pl.ds(base, 32), :]
        hot_rows = jnp.concatenate(
            [onehot(near[:, r : r + 1] == latitudes) for r in range(ROWS)], axis=0
        )
        both = jnp.dot(hot_rows, north_south[...], preferred_element_type=F32)
        parts = [
            jnp.where(
                side[:, r : r + 1] > 0.0,
                both[r * 32 : (r + 1) * 32, 0:128],
                both[r * 32 : (r + 1) * 32, 128:256],
            ).astype(BF16)
            for r in range(ROWS)
        ] + [jnp.zeros((32, 128), BF16)] * 4
        line = jnp.concatenate(
            [jnp.concatenate(parts[c * 8 : c * 8 + 8], axis=1) for c in range(3)], axis=0
        )
        piece = lax.dot_general(
            line, shuffle[...], (((1,), (1,)), ((), ())), preferred_element_type=F32
        )
        for c in range(3):
            for s in range(SLOTS):
                small[pl.ds(c * 5 + s, 32, stride=STRIDE), :] = piece[
                    c * 32 : c * 32 + 32, s * 128 : (s + 1) * 128
                ]
        for w in range(32):
            send_back[base + w] = small[w * STRIDE : w * STRIDE + 16, :].astype(BF16)

        def give(i, _, base=base):
            target = base + lax.rem(wave + i, 32)
            remote(
                send_back.at[target], land_back.at[wave], send_back_sem, recv_back_sem,
                (target, core),
            ).start()
            return 0

        if g == 0:
            own_back.start()
        lax.fori_loop(1 if g == 0 else 0, 32, give, 0)

    state_copy.wait()
    for s in range(SLOTS):
        mine = jnp.where(core == 0, state_half[0, s].astype(F32), state_half[1, s].astype(F32))
        theirs = state_land[s].astype(F32)
        none = jnp.zeros_like(mine)
        state_mine_ref[ORDER[0][s]] = jnp.where(core == 0, mine, none).astype(BF16)
        state_mine_ref[ORDER[1][s]] = jnp.where(core == 0, none, mine).astype(BF16)
        state_other_ref[ORDER[0][s]] = jnp.where(core == 0, none, theirs).astype(BF16)
        state_other_ref[ORDER[1][s]] = jnp.where(core == 0, theirs, none).astype(BF16)
    own_back.wait()
    pltpu.make_async_copy(
        send_back.at[all_but_one], land_back.at[all_but_one], send_back_sem
    ).wait()
    pltpu.make_async_copy(
        send_back.at[all_but_one], land_back.at[all_but_one], recv_back_sem
    ).wait()

    for w in range(NW):
        wide[w * STRIDE : w * STRIDE + 16, :] = land_back[w].astype(F32)
    for c in range(3):
        for s in range(SLOTS):
            left[:, c, :, s * 128 : (s + 1) * 128] = (
                jnp.transpose(wide[pl.ds(c * 5 + s, NW, stride=STRIDE), :])
                .astype(BF16)
                .reshape(2, 64, 128)
            )

    def columns(side, ref):
        for c in range(3):
            value = jnp.dot(left[side, c], hot[...], preferred_element_type=F32).astype(BF16)
            for f in range(8):
                ref[f, c * 8 : min(c * 8 + 8, ROWS), :] = value[f * 8 : f * 8 + min(8, ROWS - c * 8)]

    columns(1 - core, half)
    half_copy = remote(half, half_land, half_send, half_recv, partner)
    half_copy.start()
    columns(core, grid_mine_ref)
    half_copy.wait()
    grid_other_ref[...] = half_land[...]


def vmem():
    return pl.BlockSpec(memory_space=pltpu.VMEM)


def smem():
    return pl.BlockSpec(memory_space=pltpu.SMEM)


def run(wave_slots, matrices, x, slots, lat):
    cosine, logsin, weight, start = constants()
    pressure, depths, modes, project, heat = matrices
    dma = pltpu.SemaphoreType.DMA
    return pl.pallas_call(
        kernel,
        out_shape=(
            jax.ShapeDtypeStruct((8, ROWS, WAVES), BF16),
            jax.ShapeDtypeStruct((8, ROWS, WAVES), BF16),
            jax.ShapeDtypeStruct((2 * SLOTS, 8, WAVES), BF16),
            jax.ShapeDtypeStruct((2 * SLOTS, 8, WAVES), BF16),
        ),
        in_specs=[smem()] * 7 + [vmem()] * 6,
        out_specs=(vmem(), vmem(), vmem(), vmem()),
        scratch_shapes=[
            pltpu.VMEM((8, ROWS, WAVES), BF16),
            pltpu.VMEM((SLOTS * NW, WAVES), BF16),
            pltpu.VMEM((3, 128, WAVES), F32),
            pltpu.VMEM((NW * STRIDE, 128), F32),
            pltpu.VMEM((NW, 16, 128), BF16),
            pltpu.VMEM((NW, 16, 128), BF16),
            pltpu.VMEM((NW, 16, 128), BF16),
            pltpu.VMEM((NW, 16, 128), BF16),
            pltpu.VMEM((8, PAD), F32),
            pltpu.SMEM((8, PAD), F32),
            pltpu.VMEM((3, CHAIN, HEMI), BF16),
            pltpu.VMEM((32 * STRIDE, 128), F32),
            pltpu.VMEM((NLAT, 256), BF16),
            pltpu.VMEM((HEMI, 256), F32),
            pltpu.VMEM((PAD, 128), F32),
            pltpu.VMEM((128, PAD), F32),
            pltpu.VMEM((640, 1024), BF16),
            pltpu.VMEM((HEMI, 256), BF16),
            pltpu.VMEM((2, 128, HEMI), F32),
            pltpu.VMEM((NW, ROWS), jnp.int32),
            pltpu.VMEM((NW, ROWS), F32),
            pltpu.VMEM((32 * STRIDE, 128), F32),
            pltpu.VMEM((2, SLOTS, 8, WAVES), BF16),
            pltpu.VMEM((SLOTS, 8, WAVES), BF16),
            pltpu.VMEM((2, 3, 64, 640), BF16),
            pltpu.VMEM((8, ROWS, WAVES), BF16),
            pltpu.VMEM((8, ROWS, WAVES), BF16),
            pltpu.SemaphoreType.REGULAR,
        ]
        + [dma] * 13,
        compiler_params=pltpu.CompilerParams(
            vmem_limit_bytes=VMEM, has_side_effects=True, collective_id=1
        ),
    )(
        wave_slots, jnp.asarray(start), pressure, depths, modes, project, heat,
        x, slots, lat, jnp.asarray(cosine), jnp.asarray(logsin), jnp.asarray(weight),
    )


def body(
    fourier,
    lat_rows,
    wave_slots,
    pressure_balance_operator,
    depths,
    vertical_modes,
    mode_projection,
    heat_link_operator,
):
    matrices = (
        pressure_balance_operator, depths, vertical_modes, mode_projection, heat_link_operator,
    )
    grid, grid_other, state, state_other = run(
        wave_slots,
        matrices,
        fourier.reshape(8, ROWS, WAVES),
        wave_slots.reshape(NW, 2 * SLOTS),
        lat_rows.reshape(NW, ROWS),
    )
    return (
        (state + state_other).reshape(2 * SLOTS, 2, 2, 2, WAVES),
        (grid + grid_other).reshape(2, 2, 2, ROWS, WAVES),
    )


def solution(mesh):
    in_specs = (P(None, None, "lev", "wave", None), P(), P(), P(), P(), P(), P(), P())
    out_specs = (P("wave", None, None, "lev", None), P(None, None, "lev", "wave", None))
    return jax.shard_map(body, mesh=mesh, in_specs=in_specs, out_specs=out_specs, check_vma=False)
```

time: 119 us -> 80.8 us (0.68)
  Pallas kernels: 109 us -> 72.8 us
  local copies, waits for them, and re-layouts: 8.17 us -> 5.87 us
    pallas_call x3 -> x1, Pallas kernels: 109 us -> 72.8 us  [run(): pl.pallas_call(kernel, out_shape=(jax.ShapeDtypeStruct((8, ROWS, WAVES),...]
    gather x2 -> x0, local copies, waits for them, and re-layouts: 1.29 us -> none  [body(): own = jnp.where(core == 0, ten[np.array(ORDER[0])], ten[np.array(ORDER[1])])]
    add x0 -> x2, other arithmetic: none -> 1.28 us  [the longest x1 1.16 us: body(): state + state_other]
    unnamed x10 -> x8, local copies, waits for them, and re-layouts: 3.63 us -> 2.9 us
where the time goes in v2:
time: 80.8 us; the launch traced here: 80.6 us
  Pallas kernels  72.8 us (90%)
  local copies, waits for them, and re-layouts  5.87 us (7%)
  other arithmetic  1.28 us (2%)
    pallas_call x1, Pallas kernels, run(): pl.pallas_call(kernel, out_shape=(jax.ShapeDtypeStruct((8, ROWS, WAVES),...  72.8 us
    unnamed x8, local copies, waits for them, and re-layouts  2.9 us

profile of v2, /device:TPU:1, one launch (start us, length us, event | category | flops | bytes accessed | tf_op | source)
XLA Modules:
  0.0 80.6 jit_solution(11649010530855680589)
XLA Ops:
  0.6 0.0 copy-start.2
  0.6 1.4 %reshape.21.lat_ref = s32[128,20]{1,0:T(8,128)} reshape(s32[2560]{0:T(1024)} %param.13) | data formatting | bytes 20480 | tf_op jit(solution)/shard_map/reshape | solution.py:581
  2.1 0.0 copy-done.2
  2.1 0.8 reshape.20.slots_ref
  2.9 1.8 %copy.16 = bf16[2,2,2,20,1280]{4,3,2,1,0:T(8,128)(2,1)} copy(bf16[2,2,2,20,1280]{4,2,3,1,0:T(2,128)(2,1)} %param.12) | data formatting | bytes 819200 | tf_op args[0]
  4.7 72.8 %shard_map.131 = (bf16[8,20,1280]{2,1,0:T(8,128)(2,1)}, bf16[8,20,1280]{2,1,0:T(8,128)(2,1)}, bf16[10,8,1280]{2,1,0:T(8,128)(2,1)}, bf16[10,8,1280]{2,1,0:T(8,128)(2,1)}) custom-call(s32[1280]{0:T(1024)} %waves_ref.1, f32[1280]{0:T(1024)} %constant.8.clone.start_ref, f32[4,4]{1,0:T(4,128)} %pressure_ref.1, f32[4]{0:T(128)} %depths_ref.1, f32[4,4]{1,0:T(4,128)} %modes_ref.1, ...), custom_call_target="tpu_custom_call" | custom-call | tf_op jit(solution)/shard_map/pallas_call | solution.py:513
  77.5 0.0 copy-start
  77.5 0.0 copy-start.1
  77.5 1.2 %add.6 = bf16[10,8,1280]{2,1,0:T(8,128)(2,1)S(1)} add(bf16[10,8,1280]{2,1,0:T(8,128)(2,1)} %get-tuple-element.6, bf16[10,8,1280]{2,1,0:T(8,128)(2,1)} %get-tuple-element.7) | non-fusion elementwise | flops 102400 | bytes 614400 | tf_op jit(solution)/shard_map/add | solution.py:584
  78.6 0.8 reshape.22
  79.4 0.0 copy-done
  79.4 0.0 copy-done.1
  79.4 0.1 add.7
  79.5 1.1 %copy.17 = bf16[2,2,2,20,1280]{4,2,3,1,0:T(2,128)(2,1)} copy(bf16[2,2,2,20,1280]{4,3,2,1,0:T(8,128)(2,1)S(1)} %bitcast.3) | data formatting | bytes 819200
Async XLA Ops:
  0.6 1.5 %copy-start.2 = (s32[1280]{0:T(1024)S(1)}, s32[1280]{0:T(1024)}, u32[]{:S(2)}) copy-start(s32[1280]{0:T(1024)} %waves_ref.1) | copy-start | bytes 15364
  77.5 1.9 %copy-start = (bf16[8,20,1280]{2,1,0:T(8,128)(2,1)S(1)}, bf16[8,20,1280]{2,1,0:T(8,128)(2,1)}, u32[]{:S(2)}) copy-start(bf16[8,20,1280]{2,1,0:T(8,128)(2,1)} %get-tuple-element.8) | copy-start | bytes 1228804
  77.5 1.9 %copy-start.1 = (bf16[8,20,1280]{2,1,0:T(8,128)(2,1)S(1)}, bf16[8,20,1280]{2,1,0:T(8,128)(2,1)}, u32[]{:S(2)}) copy-start(bf16[8,20,1280]{2,1,0:T(8,128)(2,1)} %get-tuple-element.9) | copy-start | bytes 1228804

commit v3 on v2

--- a/solution.py
+++ b/solution.py
@@ -19,6 +19,8 @@
 NW = 128
 ROWS = NLAT // NW
 SLOTS = 5
+PARTS = 21
+KROWS = NW * 24
 TILES = HEMI // 128
 CHAIN = 1296
 BLOCKS = CHAIN // 16
@@ -88,11 +90,11 @@
 
 def kernel(
     waves_ref, start_ref, pressure_ref, depths_ref, modes_ref, project_ref, heat_ref,
-    x_ref, slots_ref, lat_ref, cosine_ref, logsin_ref, weight_ref,
+    x_ref, slots_ref, line_ref, cosine_ref, logsin_ref, weight_ref,
     grid_mine_ref, grid_other_ref, state_mine_ref, state_other_ref,
     other, hot, rows, wide, send, land, send_back, land_back,
-    coef_v, coef_s, table, block, folded_in, folds, spec, turned, shuffle, north_south,
-    ns_rows, mirror_ref, sign_ref, small, state_half, state_land, left, half, half_land,
+    coef_v, coef_s, table, block, folded_in, folds, spec, turned, gathered, north_south,
+    ns_rows, lat_rows, where, state_half, state_land, left, half, half_land,
     round_two, coef_sem, pair_send, pair_recv, own_sem, send_sem, recv_sem,
     state_send, state_recv, own_back_sem, send_back_sem, recv_back_sem, half_send, half_recv,
 ):
@@ -167,22 +169,18 @@
     pair = remote(x_ref, other, pair_send, pair_recv, partner)
     pair.start()
 
-    source = iota((1, 1024), 1)
-    source = (source % 128) // 16 * 128 + source % 16 * 8 + source // 128
-    valid = iota((1, 1024), 1) % 128 < 80
-    shuffle[...] = onehot(valid & (iota((640, 1024), 0) == source))
-
     def place(ref, side):
         for f in range(8):
-            value = ref[f].astype(F32)
-            at = pl.multiple_of(side * 64 + f * 8, 8)
-            rows[0, pl.ds(at, 8), :] = value[0:8]
-            rows[1, pl.ds(at, 8), :] = value[8:16]
-            rows[2, pl.ds(at, 8), :] = jnp.concatenate(
-                [value[16:20], jnp.zeros((4, WAVES), F32)], axis=0
-            )
-
+            rows[side, f * PARTS : f * PARTS + ROWS, :] = ref[f].astype(F32)
+
+    rows[...] = jnp.zeros((2, 8 * PARTS, WAVES), F32)
     place(x_ref, core)
+    for q in range(KROWS // 128):
+        lat_rows[q * 128 : (q + 1) * 128, :] = jnp.transpose(
+            jnp.broadcast_to(line_ref[q : q + 1, :].astype(F32), (128, 128))
+        )
+    lat_line = jnp.concatenate([line_ref[q : q + 1, :] for q in range(KROWS // 128)], axis=1)
+    mirror_line = jnp.minimum(lat_line, NLAT - 1 - lat_line)
 
     cosine = [cosine_ref[0:8, :]] * 3 + [cosine_ref[8:16, :]]
     logsin = [logsin_ref[0:8, :]] * 3 + [logsin_ref[8:16, :]]
@@ -244,67 +242,87 @@
 
     pair.wait()
     place(other, 1 - core)
-    wide[pl.ds(15, NW, stride=STRIDE), :] = jnp.zeros((NW, 128), F32)
-    for c in range(3):
-        arranged = lax.dot_general(
-            hot[...], rows[c].astype(BF16), (((1,), (1,)), ((), ())), preferred_element_type=F32
-        )
-        for s in range(SLOTS):
-            wide[pl.ds(c * 5 + s, NW, stride=STRIDE), :] = arranged[s * NW : (s + 1) * NW]
+    arranged = lax.dot_general(
+        rows[...].reshape(16 * PARTS, WAVES).astype(BF16),
+        hot[...],
+        (((1,), (1,)), ((), ())),
+        preferred_element_type=F32,
+    )
+    for s in range(SLOTS):
+        gathered[s] = arranged[:, s * NW : (s + 1) * NW]
+    ahead = lane < 80
+
+    def one_row(r):
+        return jnp.transpose(
+            jnp.concatenate(
+                [
+                    gathered[s, pl.ds(r, 16, stride=PARTS), :]
+                    for s in range(SLOTS)
+                ]
+                + [jnp.zeros((48, NW), F32)],
+                axis=0,
+            )
+        )
+
+    for r in range(4):
+        last = one_row(16 + r)
+        wide[pl.ds(r, NW, stride=STRIDE), :] = jnp.where(
+            ahead, one_row(r), pltpu.roll(last, 80, 1)
+        )
+        wide[pl.ds(4 + r, NW, stride=STRIDE), :] = jnp.where(
+            ahead, one_row(4 + r), pltpu.roll(last, 32, 1)
+        )
+    for r in range(8, 16):
+        wide[pl.ds(r, NW, stride=STRIDE), :] = one_row(r)
     for w in range(NW):
         send[w] = wide[w * STRIDE : w * STRIDE + 16, :].astype(BF16)
     pl.semaphore_wait(round_two, 15)
     own = pltpu.make_async_copy(send.at[wave], land.at[wave], own_sem)
     own.start()
 
-    def send_to(step):
+    def send_to(step, _):
         target = lax.rem(wave + step, NW)
         remote(send.at[target], land.at[wave], send_sem, recv_sem, (target, core)).start()
-
-    def make_and_send(i, carry):
-        send_to(2 * i + 1)
-        send_to(2 * i + 2)
-        return make(EARLY + i, carry)
-
-    carry = lax.fori_loop(0, NW // 2 - 1, make_and_send, carry)
-    send_to(NW - 1)
-    lax.fori_loop(EARLY + NW // 2 - 1, BLOCKS, make, carry)
-
-    lat = lat_ref[...]
-    sign = jnp.where(lat < HEMI, 1.0, -1.0)
-    mirror = jnp.minimum(lat, NLAT - 1 - lat)
-    mirror_rows = jnp.transpose(
-        jnp.concatenate([mirror.astype(F32), jnp.zeros((NW, 128 - ROWS), F32)], axis=1)
-    ).astype(jnp.int32)
-    mirror_line = jnp.concatenate([mirror_rows[r : r + 1, :] for r in range(ROWS)], axis=1)
-
-    mirror_ref[...] = mirror
-    sign_ref[...] = sign
+        return 0
+
+    lax.fori_loop(1, NW, send_to, 0)
+    lax.fori_loop(EARLY, BLOCKS, make, carry)
+
+    def where_from(t, _):
+        at = pl.multiple_of(t * 128, 128)
+        where[pl.ds(at, 128), :] = onehot(mirror_line == iota((128, KROWS), 0) + t * 128)
+        return 0
+
+    lax.fori_loop(0, TILES, where_from, 0)
 
     own.wait()
     all_but_one = pl.ds(0, NW - 1)
     pltpu.make_async_copy(send.at[all_but_one], land.at[all_but_one], send_sem).wait()
     pltpu.make_async_copy(send.at[all_but_one], land.at[all_but_one], recv_sem).wait()
 
-    for w in range(NW):
-        wide[w * STRIDE : w * STRIDE + 16, :] = land[w].astype(F32)
-    for c in range(3):
-        piece = jnp.concatenate(
-            [wide[pl.ds(c * 5 + s, NW, stride=STRIDE), :].astype(BF16) for s in range(SLOTS)],
-            axis=1,
-        )
-        spread = jnp.dot(piece, shuffle[...], preferred_element_type=F32)
-        for r in range(8 if c < 2 else 4):
-            at = c * 8 + r
-            part = spread[:, r * 128 : (r + 1) * 128]
-            folded_in[at * NW : (at + 1) * NW, 0:128] = part.astype(BF16)
-            folded_in[at * NW : (at + 1) * NW, 128:256] = (part * sign[:, at : at + 1]).astype(BF16)
+    received = land[...].astype(F32)
+    sub = iota((NW, 8, 128), 1)
+    lanes_of = iota((NW, 8, 128), 2)
+    tops = received[:, 0:8, :].reshape(NW * 8, 128)
+    three = pltpu.roll(tops, 48, 1).reshape(NW, 8, 128)
+    two = pltpu.roll(tops, 96, 1).reshape(NW, 8, 128)
+    late = jnp.where(
+        sub < 4,
+        jnp.where(lanes_of < 48, three, 0.0),
+        jnp.where((lanes_of >= 48) & (lanes_of < 80), two, 0.0),
+    ).reshape(NW * 8, 128)
+    early = jnp.where(ahead, received.reshape(NW * 16, 128), 0.0)
+    for at, part in ((0, early), (NW * 16, late)):
+        end = at + part.shape[0]
+        northern = lat_rows[at:end, :] < float(HEMI)
+        folded_in[at:end, 0:128] = part.astype(BF16)
+        folded_in[at:end, 128:256] = jnp.where(northern, part, -part).astype(BF16)
 
     def fold(t, _):
-        hot = onehot(mirror_line == iota((256, NLAT), 0) + t * 256)
-        total = jnp.dot(hot, folded_in[...], preferred_element_type=F32)
         at = pl.multiple_of(t * 256, 256)
-        folds[pl.ds(at, 256), :] = total
+        folds[pl.ds(at, 256), :] = jnp.dot(
+            where[pl.ds(at, 256), :], folded_in[...], preferred_element_type=F32
+        )
         return 0
 
     lax.fori_loop(0, HEMI // 256, fold, 0)
@@ -412,38 +430,38 @@
                 ns_rows[u, :, t * 128 : (t + 1) * 128]
             ).astype(BF16)
 
-    latitudes = iota((32, HEMI), 1)
-    small[pl.ds(15, 32, stride=STRIDE), :] = jnp.zeros((32, 128), F32)
+    latitudes = iota((1, HEMI), 1).astype(F32)
     own_back = pltpu.make_async_copy(send_back.at[wave], land_back.at[wave], own_back_sem)
+    sub = iota((32, 8, 128), 1)
     for g in range(4):
         base = pl.multiple_of(lax.rem(lax.div(wave, 32) + g, 4) * 32, 32)
-        near = mirror_ref[pl.ds(base, 32), :]
-        side = sign_ref[pl.ds(base, 32), :]
+        lat = jnp.concatenate(
+            [
+                lat_rows[pl.ds(pl.multiple_of(base * 16, 512), 512), :],
+                lat_rows[pl.ds(pl.multiple_of(NW * 16 + base * 8, 256), 256), :],
+            ],
+            axis=0,
+        )
+        mirror = jnp.minimum(lat, float(NLAT - 1) - lat)
         hot_rows = jnp.concatenate(
-            [onehot(near[:, r : r + 1] == latitudes) for r in range(ROWS)], axis=0
+            [
+                onehot(mirror == latitudes[:, t * 128 : (t + 1) * 128])
+                for t in range(TILES)
+            ],
+            axis=1,
         )
         both = jnp.dot(hot_rows, north_south[...], preferred_element_type=F32)
-        parts = [
-            jnp.where(
-                side[:, r : r + 1] > 0.0,
-                both[r * 32 : (r + 1) * 32, 0:128],
-                both[r * 32 : (r + 1) * 32, 128:256],
-            ).astype(BF16)
-            for r in range(ROWS)
-        ] + [jnp.zeros((32, 128), BF16)] * 4
-        line = jnp.concatenate(
-            [jnp.concatenate(parts[c * 8 : c * 8 + 8], axis=1) for c in range(3)], axis=0
-        )
-        piece = lax.dot_general(
-            line, shuffle[...], (((1,), (1,)), ((), ())), preferred_element_type=F32
-        )
-        for c in range(3):
-            for s in range(SLOTS):
-                small[pl.ds(c * 5 + s, 32, stride=STRIDE), :] = piece[
-                    c * 32 : c * 32 + 32, s * 128 : (s + 1) * 128
-                ]
-        for w in range(32):
-            send_back[base + w] = small[w * STRIDE : w * STRIDE + 16, :].astype(BF16)
+        part = jnp.where(lat < float(HEMI), both[:, 0:128], both[:, 128:256])
+        late = part[512:768]
+        late = jnp.where(
+            sub < 4,
+            pltpu.roll(late, 80, 1).reshape(32, 8, 128),
+            pltpu.roll(late, 32, 1).reshape(32, 8, 128),
+        )
+        tile = part[0:512].reshape(32, 16, 128)
+        send_back[pl.ds(base, 32)] = jnp.concatenate(
+            [jnp.where(ahead.reshape(1, 1, 128), tile[:, 0:8], late), tile[:, 8:16]], axis=1
+        ).astype(BF16)
 
         def give(i, _, base=base):
             target = base + lax.rem(wave + i, 32)
@@ -476,19 +494,27 @@
 
     for w in range(NW):
         wide[w * STRIDE : w * STRIDE + 16, :] = land_back[w].astype(F32)
-    for c in range(3):
-        for s in range(SLOTS):
-            left[:, c, :, s * 128 : (s + 1) * 128] = (
-                jnp.transpose(wide[pl.ds(c * 5 + s, NW, stride=STRIDE), :])
-                .astype(BF16)
-                .reshape(2, 64, 128)
-            )
+    for r in range(16):
+        value = jnp.transpose(wide[pl.ds(r, NW, stride=STRIDE), :])
+        blocks = [(r, s) for s in range(SLOTS)]
+        if r < 4:
+            blocks += [(16 + r, s) for s in range(3)]
+        elif r < 8:
+            blocks += [(12 + r, s) for s in range(3, SLOTS)]
+        for q, (at, s) in enumerate(blocks):
+            for v in range(2):
+                left[v, s, pl.ds(at, 8, stride=PARTS), :] = value[
+                    q * 16 + v * 8 : q * 16 + v * 8 + 8
+                ]
 
     def columns(side, ref):
-        for c in range(3):
-            value = jnp.dot(left[side, c], hot[...], preferred_element_type=F32).astype(BF16)
-            for f in range(8):
-                ref[f, c * 8 : min(c * 8 + 8, ROWS), :] = value[f * 8 : f * 8 + min(8, ROWS - c * 8)]
+        value = jnp.dot(
+            jnp.concatenate([left[side, s].astype(BF16) for s in range(SLOTS)], axis=1),
+            hot[...],
+            preferred_element_type=F32,
+        )
+        for f in range(8):
+            ref[f] = value[f * PARTS : f * PARTS + ROWS].astype(BF16)
 
     columns(1 - core, half)
     half_copy = remote(half, half_land, half_send, half_recv, partner)
@@ -506,7 +532,7 @@
     return pl.BlockSpec(memory_space=pltpu.SMEM)
 
 
-def run(wave_slots, matrices, x, slots, lat):
+def run(wave_slots, matrices, x, slots, line):
     cosine, logsin, weight, start = constants()
     pressure, depths, modes, project, heat = matrices
     dma = pltpu.SemaphoreType.DMA
@@ -523,7 +549,7 @@
         scratch_shapes=[
             pltpu.VMEM((8, ROWS, WAVES), BF16),
             pltpu.VMEM((SLOTS * NW, WAVES), BF16),
-            pltpu.VMEM((3, 128, WAVES), F32),
+            pltpu.VMEM((2, 8 * PARTS, WAVES), F32),
             pltpu.VMEM((NW * STRIDE, 128), F32),
             pltpu.VMEM((NW, 16, 128), BF16),
             pltpu.VMEM((NW, 16, 128), BF16),
@@ -533,19 +559,18 @@
             pltpu.SMEM((8, PAD), F32),
             pltpu.VMEM((3, CHAIN, HEMI), BF16),
             pltpu.VMEM((32 * STRIDE, 128), F32),
-            pltpu.VMEM((NLAT, 256), BF16),
+            pltpu.VMEM((KROWS, 256), BF16),
             pltpu.VMEM((HEMI, 256), F32),
             pltpu.VMEM((PAD, 128), F32),
             pltpu.VMEM((128, PAD), F32),
-            pltpu.VMEM((640, 1024), BF16),
+            pltpu.VMEM((SLOTS, 16 * PARTS, NW), F32),
             pltpu.VMEM((HEMI, 256), BF16),
             pltpu.VMEM((2, 128, HEMI), F32),
-            pltpu.VMEM((NW, ROWS), jnp.int32),
-            pltpu.VMEM((NW, ROWS), F32),
-            pltpu.VMEM((32 * STRIDE, 128), F32),
+            pltpu.VMEM((KROWS, 128), F32),
+            pltpu.VMEM((HEMI, KROWS), BF16),
             pltpu.VMEM((2, SLOTS, 8, WAVES), BF16),
             pltpu.VMEM((SLOTS, 8, WAVES), BF16),
-            pltpu.VMEM((2, 3, 64, 640), BF16),
+            pltpu.VMEM((2, SLOTS, 8 * PARTS, NW), F32),
             pltpu.VMEM((8, ROWS, WAVES), BF16),
             pltpu.VMEM((8, ROWS, WAVES), BF16),
             pltpu.SemaphoreType.REGULAR,
@@ -556,7 +581,7 @@
         ),
     )(
         wave_slots, jnp.asarray(start), pressure, depths, modes, project, heat,
-        x, slots, lat, jnp.asarray(cosine), jnp.asarray(logsin), jnp.asarray(weight),
+        x, slots, line, jnp.asarray(cosine), jnp.asarray(logsin), jnp.asarray(weight),
     )
 
 
@@ -573,12 +598,15 @@
     matrices = (
         pressure_balance_operator, depths, vertical_modes, mode_projection, heat_link_operator,
     )
+    by_device = lat_rows.reshape(NW, ROWS)
+    first = by_device[:, 0:16].reshape(NW * 16)
+    last = jnp.concatenate([by_device[:, 16:20]] * 2, axis=1).reshape(NW * 8)
     grid, grid_other, state, state_other = run(
         wave_slots,
         matrices,
         fourier.reshape(8, ROWS, WAVES),
         wave_slots.reshape(NW, 2 * SLOTS),
-        lat_rows.reshape(NW, ROWS),
+        jnp.concatenate([first, last]).reshape(KROWS // 128, 128),
     )
     return (
         (state + state_other).reshape(2 * SLOTS, 2, 2, 2, WAVES),

time: 80.8 us -> 74.7 us (0.925)
  Pallas kernels: 72.8 us -> 67.2 us
  local copies, waits for them, and re-layouts: 5.87 us -> 4.63 us
    pallas_call x1, Pallas kernels: 72.8 us -> 67.2 us  [run(): pl.pallas_call(kernel, out_shape=(jax.ShapeDtypeStruct((8, ROWS, WAVES),...]
    unnamed x8 -> x10, local copies, waits for them, and re-layouts: 2.9 us -> 2 us
where the time goes in v3:
time: 74.7 us; the launch traced here: 74.5 us
  Pallas kernels  67.2 us (90%)
  local copies, waits for them, and re-layouts  4.63 us (6%)
  other arithmetic  1.97 us (3%)
    pallas_call x1, Pallas kernels, run(): pl.pallas_call(kernel, out_shape=(jax.ShapeDtypeStruct((8, ROWS, WAVES),...  67.2 us
    unnamed x10, local copies, waits for them, and re-layouts  2 us

profile of v3, /device:TPU:1, one launch (start us, length us, event | category | flops | bytes accessed | tf_op | source)
XLA Modules:
  0.0 74.5 jit_solution(2924144156975311275)
XLA Ops:
  0.6 0.0 copy-start.2
  0.6 0.9 %reshape.30 = s32[128,20]{1,0:T(8,128)S(1)} reshape(s32[2560]{0:T(1024)} %param.13) | data formatting | bytes 20480 | tf_op jit(solution)/shard_map/reshape | solution.py:601
  1.5 0.1 reshape.31
  1.6 0.1 slice.9
  1.7 0.1 pad_add_fusion
  1.8 0.1 reshape.32
  1.9 0.0 copy-start.3
  1.9 0.6 add_bitcast_fusion.line_ref
  2.5 0.1 copy-done.3
  2.6 0.8 %reshape.29.slots_ref = s32[128,10]{1,0:T(8,128)} reshape(s32[1280]{0:T(1024)S(1)} %copy-done.3) | data formatting | bytes 10240 | tf_op jit(solution)/shard_map/reshape | solution.py:608
  3.3 0.0 copy-done.2
  3.3 0.8 %copy.23 = bf16[2,2,2,20,1280]{4,3,2,1,0:T(8,128)(2,1)} copy(bf16[2,2,2,20,1280]{4,2,3,1,0:T(2,128)(2,1)S(1)} %copy-done.2) | data formatting | bytes 819200 | tf_op args[0]
  4.2 67.2 %shard_map.131 = (bf16[8,20,1280]{2,1,0:T(8,128)(2,1)}, bf16[8,20,1280]{2,1,0:T(8,128)(2,1)}, bf16[10,8,1280]{2,1,0:T(8,128)(2,1)}, bf16[10,8,1280]{2,1,0:T(8,128)(2,1)}) custom-call(s32[1280]{0:T(1024)} %waves_ref.1, f32[1280]{0:T(1024)} %constant.8.clone.start_ref, f32[4,4]{1,0:T(4,128)} %pressure_ref.1, f32[4]{0:T(128)} %depths_ref.1, f32[4,4]{1,0:T(4,128)} %modes_ref.1, ...), custom_call_target="tpu_custom_call" | custom-call | tf_op jit(solution)/shard_map/pallas_call | solution.py:539
  71.3 0.0 copy-start
  71.3 0.0 copy-start.1
  71.3 1.2 %add.6 = bf16[10,8,1280]{2,1,0:T(8,128)(2,1)S(1)} add(bf16[10,8,1280]{2,1,0:T(8,128)(2,1)} %get-tuple-element.6, bf16[10,8,1280]{2,1,0:T(8,128)(2,1)} %get-tuple-element.7) | non-fusion elementwise | flops 102400 | bytes 614400 | tf_op jit(solution)/shard_map/add | solution.py:612
  72.5 0.8 %reshape.34 = bf16[10,2,2,2,1280]{4,3,2,1,0:T(2,128)(2,1)} reshape(bf16[10,8,1280]{2,1,0:T(8,128)(2,1)S(1)} %add.6) | data formatting | bytes 409600 | tf_op jit(solution)/shard_map/reshape | solution.py:612
  73.3 0.0 copy-done
  73.3 0.0 copy-done.1
  73.3 0.1 add.7
  73.4 1.1 %copy.24 = bf16[2,2,2,20,1280]{4,2,3,1,0:T(2,128)(2,1)} copy(bf16[2,2,2,20,1280]{4,3,2,1,0:T(8,128)(2,1)S(1)} %bitcast.6) | data formatting | bytes 819200
Async XLA Ops:
  0.6 2.7 %copy-start.2 = (bf16[2,2,2,20,1280]{4,2,3,1,0:T(2,128)(2,1)S(1)}, bf16[2,2,2,20,1280]{4,2,3,1,0:T(2,128)(2,1)}, u32[]{:S(2)}) copy-start(bf16[2,2,2,20,1280]{4,2,3,1,0:T(2,128)(2,1)} %param.12) | copy-start | bytes 1228804
  1.9 0.7 copy-start.3
  71.3 1.9 %copy-start = (bf16[8,20,1280]{2,1,0:T(8,128)(2,1)S(1)}, bf16[8,20,1280]{2,1,0:T(8,128)(2,1)}, u32[]{:S(2)}) copy-start(bf16[8,20,1280]{2,1,0:T(8,128)(2,1)} %get-tuple-element.8) | copy-start | bytes 1228804
  71.3 1.9 %copy-start.1 = (bf16[8,20,1280]{2,1,0:T(8,128)(2,1)S(1)}, bf16[8,20,1280]{2,1,0:T(8,128)(2,1)}, u32[]{:S(2)}) copy-start(bf16[8,20,1280]{2,1,0:T(8,128)(2,1)} %get-tuple-element.9) | copy-start | bytes 1228804

commit v4 on v3

--- a/solution.py
+++ b/solution.py
@@ -27,7 +27,7 @@
 PAD = 1408
 ORDER = ((0, 1, 2, 3, 4), (6, 7, 8, 9, 5))
 EARLY = 14
-VMEM = 60 * 1024 * 1024
+VMEM = 54 * 1024 * 1024
 STRIDE = 17
 
 
@@ -55,16 +55,25 @@
     return jnp.where(condition, 1.0, 0.0).astype(BF16)
 
 
-def slot_onehot(core, slots_ref, hot):
-    numbers = slots_ref[...]
-    waves = iota((NW, WAVES), 1)
+def columns_of(line_ref, first, count, out):
+    for q in range(count):
+        out[q * 128 : (q + 1) * 128, :] = jnp.transpose(
+            jnp.broadcast_to(line_ref[first + q : first + q + 1, :].astype(F32), (128, 128))
+        )
+
+
+def slot_onehot(core, numbers, hot):
+    waves = iota((1, WAVES), 1).astype(F32)
     for s in range(SLOTS):
         mine = jnp.where(
             core == 0,
-            numbers[:, ORDER[0][s] : ORDER[0][s] + 1],
-            numbers[:, ORDER[1][s] : ORDER[1][s] + 1],
-        )
-        hot[s * NW : (s + 1) * NW, :] = onehot(mine == waves)
+            numbers[pl.ds(ORDER[0][s], NW, stride=2 * SLOTS), :],
+            numbers[pl.ds(ORDER[1][s], NW, stride=2 * SLOTS), :],
+        )
+        for t in range(TILES):
+            hot[s * NW : (s + 1) * NW, t * 128 : (t + 1) * 128] = onehot(
+                mine == waves[:, t * 128 : (t + 1) * 128]
+            )
 
 
 def remote(src, dst, send_sem, recv_sem, device):
@@ -90,11 +99,11 @@
 
 def kernel(
     waves_ref, start_ref, pressure_ref, depths_ref, modes_ref, project_ref, heat_ref,
-    x_ref, slots_ref, line_ref, cosine_ref, logsin_ref, weight_ref,
+    x_ref, line_ref, cosine_ref, logsin_ref, weight_ref,
     grid_mine_ref, grid_other_ref, state_mine_ref, state_other_ref,
     other, hot, rows, wide, send, land, send_back, land_back,
     coef_v, coef_s, table, block, folded_in, folds, spec, turned, gathered, north_south,
-    ns_rows, lat_rows, where, state_half, state_land, left, half, half_land,
+    ns_rows, numbers, lat_rows, lat_late, where, hot_rows, state_half, state_land, left, half, half_land,
     round_two, coef_sem, pair_send, pair_recv, own_sem, send_sem, recv_sem,
     state_send, state_recv, own_back_sem, send_back_sem, recv_back_sem, half_send, half_recv,
 ):
@@ -162,7 +171,9 @@
     coef_copy = pltpu.make_async_copy(coef_v, coef_s, coef_sem)
     coef_copy.start()
 
-    slot_onehot(core, slots_ref, hot)
+    columns_of(line_ref, 0, WAVES // 128, numbers)
+    slot_onehot(core, numbers, hot)
+    columns_of(line_ref, WAVES // 128, NLAT // 128, numbers)
 
     pl.semaphore_wait(barrier, 7 + 15 + 1)
     lax.fori_loop(1, 16, pass_on, 0)
@@ -175,11 +186,21 @@
 
     rows[...] = jnp.zeros((2, 8 * PARTS, WAVES), F32)
     place(x_ref, core)
-    for q in range(KROWS // 128):
-        lat_rows[q * 128 : (q + 1) * 128, :] = jnp.transpose(
-            jnp.broadcast_to(line_ref[q : q + 1, :].astype(F32), (128, 128))
-        )
-    lat_line = jnp.concatenate([line_ref[q : q + 1, :] for q in range(KROWS // 128)], axis=1)
+    for w in range(NW):
+        last = numbers[w * ROWS + 16 : w * ROWS + 20, :]
+        lat_rows[w // 4, w % 4] = numbers[w * ROWS : w * ROWS + 16, :]
+        lat_late[w // 4, w % 4] = jnp.concatenate([last, last], axis=0)
+    lat_line = jnp.concatenate(
+        [
+            jnp.transpose(lat_rows[q * 2 : q * 2 + 2].reshape(128, 128))[0:1, :]
+            for q in range(NW // 8)
+        ]
+        + [
+            jnp.transpose(lat_late[q * 4 : q * 4 + 4].reshape(128, 128))[0:1, :]
+            for q in range(NW // 16)
+        ],
+        axis=1,
+    ).astype(jnp.int32)
     mirror_line = jnp.minimum(lat_line, NLAT - 1 - lat_line)
 
     cosine = [cosine_ref[0:8, :]] * 3 + [cosine_ref[8:16, :]]
@@ -281,7 +302,8 @@
     own.start()
 
     def send_to(step, _):
-        target = lax.rem(wave + step, NW)
+        offset = lax.rem(step, 8) * 16 + lax.div(step, 8)
+        target = lax.rem(wave + offset, NW)
         remote(send.at[target], land.at[wave], send_sem, recv_sem, (target, core)).start()
         return 0
 
@@ -294,6 +316,67 @@
         return 0
 
     lax.fori_loop(0, TILES, where_from, 0)
+
+    latitudes = iota((1, HEMI), 1).astype(F32)
+
+    def lats_at(x):
+        return jnp.concatenate(
+            [lat_rows[:, x].reshape(512, 128), lat_late[:, x].reshape(256, 128)], axis=0
+        )
+
+    def where_to(x, _):
+        lat = lats_at(x)
+        mirror = jnp.minimum(lat, float(NLAT - 1) - lat)
+        for t in range(TILES):
+            hot_rows[x, :, t * 128 : (t + 1) * 128] = onehot(
+                mirror == latitudes[:, t * 128 : (t + 1) * 128]
+            )
+        return 0
+
+    lax.fori_loop(0, 4, where_to, 0)
+
+    chain_of = lane // 32
+
+    def lanes(values):
+        return jnp.where(chain_of == 0, values[0], jnp.where(chain_of == 1, values[1], values[2]))
+
+    is_second = (lane // 16) % 2 == 1
+    lane_begin = lanes(begins)
+    offset = jnp.where(is_second, lanes(seconds) - lane_begin, lanes(firsts))
+    level = (lane // 8) % 2 * 2 + lane % 2
+    field = (lane // 2) % 2
+    depth = jnp.zeros((1, 128), F32)
+    for a in range(4):
+        depth = jnp.where(level == a, depths_ref[a], depth)
+    across, down = iota((128, 128), 1), iota((128, 128), 0)
+    same = (across // 16 == down // 16) & ((across // 4) % 2 == (down // 4) % 2)
+    level_to, level_from = (across // 8) % 2 * 2 + across % 2, (down // 8) % 2 * 2 + down % 2
+    field_to, field_from = (across // 2) % 2, (down // 2) % 2
+
+    def matrix(entry, to, of):
+        total = jnp.zeros((128, 128), F32)
+        for a in range(4):
+            for b in range(4):
+                total = jnp.where((level_to == a) & (level_from == b), entry(a, b), total)
+        return jnp.where(same & (field_to == to) & (field_from == of), total, 0.0)
+
+    def product(one, two):
+        return lambda a, b: sum(one[a, e] * two[e, b] for e in range(4))
+
+    first_matrix = jnp.concatenate(
+        [
+            matrix(lambda a, b: project_ref[a, b], 0, 0),
+            matrix(product(project_ref, pressure_ref), 0, 1),
+        ],
+        axis=1,
+    )
+    second_matrix = matrix(lambda a, b: modes_ref[a, b], 0, 0) - matrix(
+        product(heat_ref, modes_ref), 1, 0
+    )
+    first_parts, second_parts = split(first_matrix), split(second_matrix)
+    turned[:, CHAIN - 16 : PAD] = jnp.zeros((128, PAD - CHAIN + 16), F32)
+    spec[CHAIN - 16 : PAD, :] = jnp.zeros((PAD - CHAIN + 16, 128), F32)
+    ns_rows[:, 96:128, :] = jnp.zeros((2, 32, HEMI), F32)
 
     own.wait()
     all_but_one = pl.ds(0, NW - 1)
@@ -312,9 +395,9 @@
         jnp.where((lanes_of >= 48) & (lanes_of < 80), two, 0.0),
     ).reshape(NW * 8, 128)
     early = jnp.where(ahead, received.reshape(NW * 16, 128), 0.0)
-    for at, part in ((0, early), (NW * 16, late)):
+    for at, part, lats in ((0, early, lat_rows), (NW * 16, late, lat_late)):
         end = at + part.shape[0]
-        northern = lat_rows[at:end, :] < float(HEMI)
+        northern = lats[...].reshape(part.shape) < float(HEMI)
         folded_in[at:end, 0:128] = part.astype(BF16)
         folded_in[at:end, 128:256] = jnp.where(northern, part, -part).astype(BF16)
 
@@ -331,47 +414,6 @@
             folds[t * 128 : (t + 1) * 128, :] * weight_ref[:, t : t + 1]
         ).astype(BF16)
 
-    chain_of = lane // 32
-
-    def lanes(values):
-        return jnp.where(chain_of == 0, values[0], jnp.where(chain_of == 1, values[1], values[2]))
-
-    is_second = (lane // 16) % 2 == 1
-    lane_begin = lanes(begins)
-    offset = jnp.where(is_second, lanes(seconds) - lane_begin, lanes(firsts))
-    level = (lane // 8) % 2 * 2 + lane % 2
-    field = (lane // 2) % 2
-    depth = jnp.zeros((1, 128), F32)
-    for a in range(4):
-        depth = jnp.where(level == a, depths_ref[a], depth)
-    across, down = iota((128, 128), 1), iota((128, 128), 0)
-    same = (across // 16 == down // 16) & ((across // 4) % 2 == (down // 4) % 2)
-    level_to, level_from = (across // 8) % 2 * 2 + across % 2, (down // 8) % 2 * 2 + down % 2
-    field_to, field_from = (across // 2) % 2, (down // 2) % 2
-
-    def matrix(entry, to, of):
-        total = jnp.zeros((128, 128), F32)
-        for a in range(4):
-            for b in range(4):
-                total = jnp.where((level_to == a) & (level_from == b), entry(a, b), total)
-        return jnp.where(same & (field_to == to) & (field_from == of), total, 0.0)
-
-    def product(one, two):
-        return lambda a, b: sum(one[a, e] * two[e, b] for e in range(4))
-
-    first_matrix = jnp.concatenate(
-        [
-            matrix(lambda a, b: project_ref[a, b], 0, 0),
-            matrix(product(project_ref, pressure_ref), 0, 1),
-        ],
-        axis=1,
-    )
-    second_matrix = matrix(lambda a, b: modes_ref[a, b], 0, 0) - matrix(
-        product(heat_ref, modes_ref), 1, 0
-    )
-    first_parts, second_parts = split(first_matrix), split(second_matrix)
-    turned[:, CHAIN - 16 : PAD] = jnp.zeros((128, PAD - CHAIN + 16), F32)
-    spec[CHAIN - 16 : PAD, :] = jnp.zeros((PAD - CHAIN + 16, 128), F32)
     step_rows = CHAIN // 3
 
     def solve(q, _):
@@ -411,7 +453,6 @@
 
     even = iota((1, CHAIN), 1) % 2 == 0
     inverse_scale = 1.0 / math.sqrt(WAVES)
-    ns_rows[:, 96:128, :] = jnp.zeros((2, 32, HEMI), F32)
     for c in range(3):
         state = turned[c * 32 : c * 32 + 32, 0:CHAIN]
         both_parities = jnp.concatenate(
@@ -430,27 +471,12 @@
                 ns_rows[u, :, t * 128 : (t + 1) * 128]
             ).astype(BF16)
 
-    latitudes = iota((1, HEMI), 1).astype(F32)
     own_back = pltpu.make_async_copy(send_back.at[wave], land_back.at[wave], own_back_sem)
     sub = iota((32, 8, 128), 1)
     for g in range(4):
-        base = pl.multiple_of(lax.rem(lax.div(wave, 32) + g, 4) * 32, 32)
-        lat = jnp.concatenate(
-            [
-                lat_rows[pl.ds(pl.multiple_of(base * 16, 512), 512), :],
-                lat_rows[pl.ds(pl.multiple_of(NW * 16 + base * 8, 256), 256), :],
-            ],
-            axis=0,
-        )
-        mirror = jnp.minimum(lat, float(NLAT - 1) - lat)
-        hot_rows = jnp.concatenate(
-            [
-                onehot(mirror == latitudes[:, t * 128 : (t + 1) * 128])
-                for t in range(TILES)
-            ],
-            axis=1,
-        )
-        both = jnp.dot(hot_rows, north_south[...], preferred_element_type=F32)
+        x = lax.rem(wave + g, 4)
+        lat = lats_at(x)
+        both = jnp.dot(hot_rows[x], north_south[...], preferred_element_type=F32)
         part = jnp.where(lat < float(HEMI), both[:, 0:128], both[:, 128:256])
         late = part[512:768]
         late = jnp.where(
@@ -459,12 +485,15 @@
             pltpu.roll(late, 32, 1).reshape(32, 8, 128),
         )
         tile = part[0:512].reshape(32, 16, 128)
-        send_back[pl.ds(base, 32)] = jnp.concatenate(
+        tile = jnp.concatenate(
             [jnp.where(ahead.reshape(1, 1, 128), tile[:, 0:8], late), tile[:, 8:16]], axis=1
         ).astype(BF16)
-
-        def give(i, _, base=base):
-            target = base + lax.rem(wave + i, 32)
+        for i in range(32):
+            send_back[i * 4 + x] = tile[i]
+
+        def give(i, _, x=x):
+            offset = lax.rem(i, 8) * 4 + lax.div(i, 8)
+            target = lax.rem(lax.div(wave, 4) + offset, 32) * 4 + x
             remote(
                 send_back.at[target], land_back.at[wave], send_back_sem, recv_back_sem,
                 (target, core),
@@ -532,7 +561,7 @@
     return pl.BlockSpec(memory_space=pltpu.SMEM)
 
 
-def run(wave_slots, matrices, x, slots, line):
+def run(wave_slots, matrices, x, line):
     cosine, logsin, weight, start = constants()
     pressure, depths, modes, project, heat = matrices
     dma = pltpu.SemaphoreType.DMA
@@ -544,7 +573,7 @@
             jax.ShapeDtypeStruct((2 * SLOTS, 8, WAVES), BF16),
             jax.ShapeDtypeStruct((2 * SLOTS, 8, WAVES), BF16),
         ),
-        in_specs=[smem()] * 7 + [vmem()] * 6,
+        in_specs=[smem()] * 7 + [vmem()] * 5,
         out_specs=(vmem(), vmem(), vmem(), vmem()),
         scratch_shapes=[
             pltpu.VMEM((8, ROWS, WAVES), BF16),
@@ -566,8 +595,11 @@
             pltpu.VMEM((SLOTS, 16 * PARTS, NW), F32),
             pltpu.VMEM((HEMI, 256), BF16),
             pltpu.VMEM((2, 128, HEMI), F32),
-            pltpu.VMEM((KROWS, 128), F32),
+            pltpu.VMEM((NLAT, 128), F32),
+            pltpu.VMEM((32, 4, 16, 128), F32),
+            pltpu.VMEM((32, 4, 8, 128), F32),
             pltpu.VMEM((HEMI, KROWS), BF16),
+            pltpu.VMEM((4, KROWS // 4, HEMI), BF16),
             pltpu.VMEM((2, SLOTS, 8, WAVES), BF16),
             pltpu.VMEM((SLOTS, 8, WAVES), BF16),
             pltpu.VMEM((2, SLOTS, 8 * PARTS, NW), F32),
@@ -581,7 +613,7 @@
         ),
     )(
         wave_slots, jnp.asarray(start), pressure, depths, modes, project, heat,
-        x, slots, line, jnp.asarray(cosine), jnp.asarray(logsin), jnp.asarray(weight),
+        x, line, jnp.asarray(cosine), jnp.asarray(logsin), jnp.asarray(weight),
     )
 
 
@@ -598,15 +630,11 @@
     matrices = (
         pressure_balance_operator, depths, vertical_modes, mode_projection, heat_link_operator,
     )
-    by_device = lat_rows.reshape(NW, ROWS)
-    first = by_device[:, 0:16].reshape(NW * 16)
-    last = jnp.concatenate([by_device[:, 16:20]] * 2, axis=1).reshape(NW * 8)
     grid, grid_other, state, state_other = run(
         wave_slots,
         matrices,
         fourier.reshape(8, ROWS, WAVES),
-        wave_slots.reshape(NW, 2 * SLOTS),
-        jnp.concatenate([first, last]).reshape(KROWS // 128, 128),
+        jnp.concatenate([wave_slots, lat_rows]).reshape((WAVES + NLAT) // 128, 128),
     )
     return (
         (state + state_other).reshape(2 * SLOTS, 2, 2, 2, WAVES),

time: 74.7 us -> 69.7 us (0.933)
  Pallas kernels: 67.2 us -> 62.6 us
  local copies, waits for them, and re-layouts: 4.63 us -> 3.66 us
    pallas_call x1, Pallas kernels: 67.2 us -> 62.6 us  [run(): pl.pallas_call(kernel, out_shape=(jax.ShapeDtypeStruct((8, ROWS, WAVES),...]
    reshape x4 -> x0, local copies, waits for them, and re-layouts: 1.79 us -> none  [the longest x1 0.86 us: body(): by_device = lat_rows.reshape(NW, ROWS)]
    unnamed x10 -> x6, local copies, waits for them, and re-layouts: 2 us -> 2.9 us
where the time goes in v4:
time: 69.7 us; the launch traced here: 69.5 us
  Pallas kernels  62.6 us (90%)
  local copies, waits for them, and re-layouts  3.66 us (5%)
  other arithmetic  2.6 us (4%)
    pallas_call x1, Pallas kernels, run(): pl.pallas_call(kernel, out_shape=(jax.ShapeDtypeStruct((8, ROWS, WAVES),...  62.6 us
    unnamed x6, local copies, waits for them, and re-layouts  2.9 us

profile of v4, /device:TPU:1, one launch (start us, length us, event | category | flops | bytes accessed | tf_op | source)
XLA Modules:
  0.0 69.5 jit_solution(10588234042926082927)
XLA Ops:
  0.6 1.3 %add_bitcast_fusion.line_ref = s32[30,128]{1,0:T(8,128)} fusion(s32[2560]{0:T(1024)} %param.13, s32[1280]{0:T(1024)} %waves_ref.1), kind=kLoop, calls=%fused_computation | loop fusion | flops 3840 | bytes 30720 | tf_op jit(solution)/shard_map/reshape | solution.py:637
  2.0 1.8 %copy.14 = bf16[2,2,2,20,1280]{4,3,2,1,0:T(8,128)(2,1)} copy(bf16[2,2,2,20,1280]{4,2,3,1,0:T(2,128)(2,1)} %param.12) | data formatting | bytes 819200 | tf_op args[0]
  3.8 62.6 %shard_map.131 = (bf16[8,20,1280]{2,1,0:T(8,128)(2,1)}, bf16[8,20,1280]{2,1,0:T(8,128)(2,1)}, bf16[10,8,1280]{2,1,0:T(8,128)(2,1)}, bf16[10,8,1280]{2,1,0:T(8,128)(2,1)}) custom-call(s32[1280]{0:T(1024)} %waves_ref.1, f32[1280]{0:T(1024)} %constant.8.clone.start_ref, f32[4,4]{1,0:T(4,128)} %pressure_ref.1, f32[4]{0:T(128)} %depths_ref.1, f32[4,4]{1,0:T(4,128)} %modes_ref.1, ...), custom_call_target="tpu_custom_call" | custom-call | tf_op jit(solution)/shard_map/pallas_call | solution.py:568
  66.4 0.0 copy-start
  66.4 0.0 copy-start.1
  66.4 1.2 %add.6 = bf16[10,8,1280]{2,1,0:T(8,128)(2,1)S(1)} add(bf16[10,8,1280]{2,1,0:T(8,128)(2,1)} %get-tuple-element.6, bf16[10,8,1280]{2,1,0:T(8,128)(2,1)} %get-tuple-element.7) | non-fusion elementwise | flops 102400 | bytes 614400 | tf_op jit(solution)/shard_map/add | solution.py:640
  67.5 0.8 %reshape.18 = bf16[10,2,2,2,1280]{4,3,2,1,0:T(2,128)(2,1)} reshape(bf16[10,8,1280]{2,1,0:T(8,128)(2,1)S(1)} %add.6) | data formatting | bytes 409600 | tf_op jit(solution)/shard_map/reshape | solution.py:640
  68.3 0.0 copy-done
  68.3 0.0 copy-done.1
  68.3 0.1 add.7
  68.4 1.1 %copy.15 = bf16[2,2,2,20,1280]{4,2,3,1,0:T(2,128)(2,1)} copy(bf16[2,2,2,20,1280]{4,3,2,1,0:T(8,128)(2,1)S(1)} %bitcast.5) | data formatting | bytes 819200
Async XLA Ops:
  66.4 1.9 %copy-start = (bf16[8,20,1280]{2,1,0:T(8,128)(2,1)S(1)}, bf16[8,20,1280]{2,1,0:T(8,128)(2,1)}, u32[]{:S(2)}) copy-start(bf16[8,20,1280]{2,1,0:T(8,128)(2,1)} %get-tuple-element.8) | copy-start | bytes 1228804
  66.4 1.9 %copy-start.1 = (bf16[8,20,1280]{2,1,0:T(8,128)(2,1)S(1)}, bf16[8,20,1280]{2,1,0:T(8,128)(2,1)}, u32[]{:S(2)}) copy-start(bf16[8,20,1280]{2,1,0:T(8,128)(2,1)} %get-tuple-element.9) | copy-start | bytes 1228804

commit v5 on v4

--- a/solution.py
+++ b/solution.py
@@ -55,10 +55,10 @@
     return jnp.where(condition, 1.0, 0.0).astype(BF16)
 
 
-def columns_of(line_ref, first, count, out):
+def columns_of(line_ref, count, out):
     for q in range(count):
         out[q * 128 : (q + 1) * 128, :] = jnp.transpose(
-            jnp.broadcast_to(line_ref[first + q : first + q + 1, :].astype(F32), (128, 128))
+            jnp.broadcast_to(line_ref[q : q + 1, :].astype(F32), (128, 128))
         )
 
 
@@ -99,7 +99,7 @@
 
 def kernel(
     waves_ref, start_ref, pressure_ref, depths_ref, modes_ref, project_ref, heat_ref,
-    x_ref, line_ref, cosine_ref, logsin_ref, weight_ref,
+    x_ref, slots_ref, lats_ref, cosine_ref, logsin_ref, weight_ref,
     grid_mine_ref, grid_other_ref, state_mine_ref, state_other_ref,
     other, hot, rows, wide, send, land, send_back, land_back,
     coef_v, coef_s, table, block, folded_in, folds, spec, turned, gathered, north_south,
@@ -171,9 +171,9 @@
     coef_copy = pltpu.make_async_copy(coef_v, coef_s, coef_sem)
     coef_copy.start()
 
-    columns_of(line_ref, 0, WAVES // 128, numbers)
+    columns_of(slots_ref, WAVES // 128, numbers)
     slot_onehot(core, numbers, hot)
-    columns_of(line_ref, WAVES // 128, NLAT // 128, numbers)
+    columns_of(lats_ref, NLAT // 128, numbers)
 
     pl.semaphore_wait(barrier, 7 + 15 + 1)
     lax.fori_loop(1, 16, pass_on, 0)
@@ -561,7 +561,7 @@
     return pl.BlockSpec(memory_space=pltpu.SMEM)
 
 
-def run(wave_slots, matrices, x, line):
+def run(wave_slots, matrices, x, slots, lats):
     cosine, logsin, weight, start = constants()
     pressure, depths, modes, project, heat = matrices
     dma = pltpu.SemaphoreType.DMA
@@ -573,7 +573,7 @@
             jax.ShapeDtypeStruct((2 * SLOTS, 8, WAVES), BF16),
             jax.ShapeDtypeStruct((2 * SLOTS, 8, WAVES), BF16),
         ),
-        in_specs=[smem()] * 7 + [vmem()] * 5,
+        in_specs=[smem()] * 7 + [vmem()] * 6,
         out_specs=(vmem(), vmem(), vmem(), vmem()),
         scratch_shapes=[
             pltpu.VMEM((8, ROWS, WAVES), BF16),
@@ -613,7 +613,7 @@
         ),
     )(
         wave_slots, jnp.asarray(start), pressure, depths, modes, project, heat,
-        x, line, jnp.asarray(cosine), jnp.asarray(logsin), jnp.asarray(weight),
+        x, slots, lats, jnp.asarray(cosine), jnp.asarray(logsin), jnp.asarray(weight),
     )
 
 
@@ -634,7 +634,8 @@
         wave_slots,
         matrices,
         fourier.reshape(8, ROWS, WAVES),
-        jnp.concatenate([wave_slots, lat_rows]).reshape((WAVES + NLAT) // 128, 128),
+        wave_slots.reshape(WAVES // 128, 128),
+        lat_rows.reshape(NLAT // 128, 128),
     )
     return (
         (state + state_other).reshape(2 * SLOTS, 2, 2, 2, WAVES),

time: 69.7 us -> 68.3 us (0.980)
  other arithmetic: 2.6 us -> 1.28 us
    reshape x1 -> x0, other arithmetic: 1.32 us -> none  [body(): jnp.concatenate([wave_slots, lat_rows]).reshape((WAVES + NLAT) // 128, 128)]
where the time goes in v5:
time: 68.3 us; the launch traced here: 68.2 us
  Pallas kernels  62.6 us (92%)
  local copies, waits for them, and re-layouts  3.66 us (5%)
  other arithmetic  1.28 us (2%)
    pallas_call x1, Pallas kernels, run(): pl.pallas_call(kernel, out_shape=(jax.ShapeDtypeStruct((8, ROWS, WAVES),...  62.6 us
    unnamed x6, local copies, waits for them, and re-layouts  2.91 us

profile of v5, /device:TPU:1, one launch (start us, length us, event | category | flops | bytes accessed | tf_op | source)
XLA Modules:
  0.0 68.2 jit_solution(13611528905658294089)
XLA Ops:
  0.6 1.8 %copy.14 = bf16[2,2,2,20,1280]{4,3,2,1,0:T(8,128)(2,1)} copy(bf16[2,2,2,20,1280]{4,2,3,1,0:T(2,128)(2,1)} %param.12) | data formatting | bytes 819200 | tf_op args[0]
  2.5 62.6 %shard_map.131 = (bf16[8,20,1280]{2,1,0:T(8,128)(2,1)}, bf16[8,20,1280]{2,1,0:T(8,128)(2,1)}, bf16[10,8,1280]{2,1,0:T(8,128)(2,1)}, bf16[10,8,1280]{2,1,0:T(8,128)(2,1)}) custom-call(s32[1280]{0:T(1024)} %waves_ref.1, f32[1280]{0:T(1024)} %constant.8.clone.start_ref, f32[4,4]{1,0:T(4,128)} %pressure_ref.1, f32[4]{0:T(128)} %depths_ref.1, f32[4,4]{1,0:T(4,128)} %modes_ref.1, ...), custom_call_target="tpu_custom_call" | custom-call | tf_op jit(solution)/shard_map/pallas_call | solution.py:568
  65.0 0.0 copy-start
  65.0 0.0 copy-start.1
  65.1 1.2 %add.6 = bf16[10,8,1280]{2,1,0:T(8,128)(2,1)S(1)} add(bf16[10,8,1280]{2,1,0:T(8,128)(2,1)} %get-tuple-element.6, bf16[10,8,1280]{2,1,0:T(8,128)(2,1)} %get-tuple-element.7) | non-fusion elementwise | flops 102400 | bytes 614400 | tf_op jit(solution)/shard_map/add | solution.py:641
  66.2 0.8 %reshape.22 = bf16[10,2,2,2,1280]{4,3,2,1,0:T(2,128)(2,1)} reshape(bf16[10,8,1280]{2,1,0:T(8,128)(2,1)S(1)} %add.6) | data formatting | bytes 409600 | tf_op jit(solution)/shard_map/reshape | solution.py:641
  67.0 0.0 copy-done
  67.0 0.0 copy-done.1
  67.0 0.1 add.7
  67.1 1.1 %copy.15 = bf16[2,2,2,20,1280]{4,2,3,1,0:T(2,128)(2,1)} copy(bf16[2,2,2,20,1280]{4,3,2,1,0:T(8,128)(2,1)S(1)} %bitcast.5) | data formatting | bytes 819200
Async XLA Ops:
  65.0 1.9 %copy-start = (bf16[8,20,1280]{2,1,0:T(8,128)(2,1)S(1)}, bf16[8,20,1280]{2,1,0:T(8,128)(2,1)}, u32[]{:S(2)}) copy-start(bf16[8,20,1280]{2,1,0:T(8,128)(2,1)} %get-tuple-element.8) | copy-start | bytes 1228804
  65.0 1.9 %copy-start.1 = (bf16[8,20,1280]{2,1,0:T(8,128)(2,1)S(1)}, bf16[8,20,1280]{2,1,0:T(8,128)(2,1)}, u32[]{:S(2)}) copy-start(bf16[8,20,1280]{2,1,0:T(8,128)(2,1)} %get-tuple-element.9) | copy-start | bytes 1228804
